TPU v7x, 1024 devices: a whole 4x8x16 slice. The times are simulated.
1024 devices in a mesh: layer: 8 (over x, core), row: 8 (over z_lo), col: 16 (over y, z_hi).
Axes of the slice: x: 4, y: 8, z: 16 (z_hi: 2, z_lo: 8; z = z_hi * 8 + z_lo), core: 2. Of those that a mesh axis runs over, the one named last changes fastest.
Arguments:
- phi_row: bfloat16 [16384, 256, 128], P(('layer', 'row', 'col')), may hold values from -6 to 6
- phi_col: bfloat16 [16384, 256, 128], P(('layer', 'row', 'col')), may hold values from -6 to 6
- weights: float32 [16384, 256], P(('layer', 'row', 'col')), may hold values from 0.2 to 300, as said below
- batch_route: int32 [16384, 1], P(('layer', 'row', 'col')), may hold values from 0 to 15; in each aligned block of 16 rows (0 to 15, 16 to 31, ...) at most 2 rows name the same one
- batch_slot: int32 [16384], P(('layer', 'row', 'col')), may hold values from 0 to 7
- ham_pattern: int32 [1024, 8], P(('layer', 'row', 'col')), may hold values 0 or 1
- dens_pattern: int32 [1024, 8], P(('layer', 'row', 'col')), may hold values 0 or 1
Outputs:
- density: bfloat16 [131072, 1024], P(('layer', 'row', 'col'))
- grid_density: float32 [16384, 256], P(('layer', 'row', 'col'))
Inputs may be any that keep to these rules, and one draw needn't show every extreme that they name: `batch_route`: batch b targets block row o - (o mod 16) + this value, o its owning device; among the rows of one device each value appears at most 2 times. `weights`: positive.
All inputs are finite; a program needn't handle non-finite values. No bound on the sum of `ham_pattern` or of `dens_pattern` on one device may be relied on, other than what follows from the above.
Results may differ from a plain program's by a relative error of at most 0.014.
Values may be sent and summed in bfloat16 or wider, within the bound.
No kernel may reach another device: no remote copies, remote signals or barrier semaphores. Data moves between devices by JAX's collectives and lax.ppermute only.
A program may use at most 128 MiB of HBM per device.

v0:
```python
import jax
import jax.numpy as jnp
from jax import lax
from jax.sharding import PartitionSpec as P


def passed_along(value, axis, steps):
    count = lax.axis_size(axis)
    first, last = (max(0, -steps), min(count, count - steps))
    return lax.ppermute(value, axis, [(source, source + steps) for source in range(first, last)])


def column_mask(switch_flags, block_width):
    shaped = jnp.broadcast_to(
        switch_flags.astype(jnp.float32)[..., :, None], switch_flags.shape + (block_width,)
    )
    return shaped.reshape(switch_flags.shape[:-1] + (switch_flags.shape[-1] * block_width,))


def unit_row(block_width, band_slots):
    columns = jnp.arange(band_slots * block_width, dtype=jnp.int32)[None, :]
    wanted = (jnp.arange(block_width, dtype=jnp.int32) + band_slots // 2 * block_width)[:, None]
    return (columns == wanted).astype(jnp.float32)


def band_rows(window, left_row):
    block_width = left_row.shape[0]
    band_slots = window.shape[0]
    half_band = band_slots // 2
    padded = jnp.pad(window, ((0, 0), (0, 0), (half_band * block_width, half_band * block_width)))
    pieces = [
        padded[
            shift_id,
            :,
            (band_slots - shift_id) * block_width : (2 * band_slots - shift_id) * block_width,
        ]
        for shift_id in range(band_slots)
    ]
    stacked = jnp.concatenate(pieces, axis=0)
    return jnp.dot(left_row, stacked, preferred_element_type=jnp.float32)


def near_span(band_slots):
    return (0, band_slots)


def widen(piece, lowest_slot, highest_slot, band_slots, block_width):
    return jnp.pad(
        piece, ((0, 0), (lowest_slot * block_width, (band_slots - highest_slot) * block_width))
    )


def fetch_near(matrix, lowest, highest, band_slots):
    block_width = matrix.shape[0]
    placed = []
    for offset in range(lowest, highest + 1):
        if offset == 0:
            placed.append(matrix)
        else:
            first_slot, after_slot = near_span(band_slots)
            piece = matrix[:, first_slot * block_width : after_slot * block_width]
            moved = passed_along(piece, ("layer", "row", "col"), -offset)
            placed.append(widen(moved, first_slot, after_slot, band_slots, block_width))
    return jnp.stack(placed)


def shards(phi_row, phi_col, weights, batch_route, batch_slot, ham_pattern, dens_pattern):
    batches, points, block_width = phi_row.shape
    band_slots = ham_pattern.shape[1]
    half_band = band_slots // 2
    groups = lax.axis_size("col")
    capacity = 2 * batches // groups
    rows_all = lax.axis_size(("layer", "row", "col"))
    own_index = lax.axis_index(("layer", "row", "col"))
    scaled = (weights[:, :, None] * phi_col.astype(jnp.float32)).astype(jnp.bfloat16)
    contrib = (
        lax.dot_general(
            phi_row, scaled, (((1,), (1,)), ((0,), (0,))), preferred_element_type=jnp.float32
        )
        / points
    )
    contrib = contrib.astype(jnp.bfloat16).reshape(batches, block_width * block_width)
    target = batch_route[:, 0]
    matches = (target[:, None] == jnp.arange(groups, dtype=jnp.int32)[None, :]).astype(jnp.int32)
    ranking = jnp.sum((jnp.cumsum(matches, axis=0) - matches) * matches, axis=1)
    position = target * capacity + ranking
    select = position[None, :] == jnp.arange(groups * capacity, dtype=jnp.int32)[:, None]
    outgoing = jnp.dot(
        select.astype(jnp.bfloat16), contrib, preferred_element_type=jnp.float32
    ).astype(jnp.bfloat16)
    labels = jnp.sum(jnp.where(select, batch_slot[None, :] + 1, 0), axis=1) - 1
    arrived, arrived_labels = (
        lax.all_to_all(outgoing, "col", split_axis=0, concat_axis=0, tiled=True),
        lax.all_to_all(labels, "col", split_axis=0, concat_axis=0, tiled=True),
    )
    placing = arrived_labels[None, :] == jnp.arange(band_slots, dtype=jnp.int32)[:, None]
    summed = jnp.dot(placing.astype(jnp.bfloat16), arrived, preferred_element_type=jnp.float32)
    summed = (
        summed.reshape(band_slots, block_width, block_width)
        .transpose(1, 0, 2)
        .reshape(block_width, band_slots * block_width)
    )
    columns = own_index + jnp.arange(band_slots, dtype=jnp.int32) - half_band
    usable = ((columns >= 0) & (columns < rows_all)).astype(jnp.int32) * ham_pattern[0]
    hamiltonian = (summed * column_mask(usable, block_width)[None, :]).astype(jnp.bfloat16)
    ham_f32 = hamiltonian.astype(jnp.float32)
    trace_part = jnp.trace(ham_f32[:, half_band * block_width : (half_band + 1) * block_width])
    square_part = jnp.sum(ham_f32 * ham_f32)
    trace_all, square_all = lax.psum((trace_part, square_part), ("layer", "row", "col"))
    mat_order = rows_all * block_width
    average = trace_all / mat_order
    spread = jnp.sqrt(square_all / mat_order - average * average + 1e-06)
    diag_lift = 0.5 + average / (4.0 * spread)
    scaling = 1.0 / (4.0 * spread)
    identity = unit_row(block_width, band_slots)
    dens_mask = column_mask(dens_pattern[0], block_width)[None, :]
    stacked = hamiltonian[None]
    row_count = stacked.shape[0]
    offsets = own_index + jnp.arange(row_count, dtype=jnp.int32)
    inside = ((offsets >= 0) & (offsets < rows_all)).astype(jnp.float32)
    made = (diag_lift * identity[None] - scaling * stacked.astype(jnp.float32)) * inside[
        :, None, None
    ]
    start_own = made.astype(jnp.bfloat16)[0]
    start_near = fetch_near(start_own, -half_band, half_band - 1, band_slots)
    purified_one = (band_rows(start_near, start_near[half_band]) * dens_mask).astype(jnp.bfloat16)
    first_near = fetch_near(purified_one, -half_band, half_band - 1, band_slots)
    square_two = band_rows(first_near, purified_one)
    density = ((2.0 * purified_one.astype(jnp.float32) - square_two) * dens_mask).astype(
        jnp.bfloat16
    )
    dense_blocks = (
        density.reshape(block_width, band_slots, block_width)
        .transpose(1, 0, 2)
        .reshape(band_slots, block_width * block_width)
    )
    answers = jnp.dot(
        placing.T.astype(jnp.bfloat16), dense_blocks, preferred_element_type=jnp.float32
    ).astype(jnp.bfloat16)
    returned = lax.all_to_all(answers, "col", split_axis=0, concat_axis=0, tiled=True)
    own_blocks = jnp.dot(
        select.T.astype(jnp.bfloat16), returned, preferred_element_type=jnp.float32
    ).astype(jnp.bfloat16)
    own_blocks = own_blocks.reshape(batches, block_width, block_width)
    partial_value = lax.dot_general(
        phi_row, own_blocks, (((2,), (1,)), ((0,), (0,))), preferred_element_type=jnp.float32
    )
    grid_density = jnp.sum(partial_value * phi_col.astype(jnp.float32), axis=2)
    return (density, grid_density)


def solution(mesh):
    in_specs = (
        P(("layer", "row", "col"), None, None),
        P(("layer", "row", "col"), None, None),
        P(("layer", "row", "col"), None),
        P(("layer", "row", "col"), None),
        P(("layer", "row", "col")),
        P(("layer", "row", "col"), None),
        P(("layer", "row", "col"), None),
    )
    out_specs = (P(("layer", "row", "col"), None), P(("layer", "row", "col"), None))
    return jax.shard_map(shards, mesh=mesh, in_specs=in_specs, out_specs=out_specs, check_vma=False)
```

profile of v0, /device:TPU:132, one launch (start us, length us, event | category | flops | bytes accessed | tf_op | source)
XLA Modules:
  0.0 620.5 jit_solution(4283062685646467079)
XLA Ops:
  0.7 0.8 fusion.48
  1.5 0.8 select_reduce_fusion.1
  2.3 0.7 multiply_add_fusion
  3.1 0.7 sub.35
  3.8 22.3 %all-to-all-start = ((s32[16,2,1]{1,2,0:T(1,128)}), s32[16,2,1]{1,2,0:T(1,128)S(1)}, u32[]{:S(2)}, u32[]{:S(2)}) async-start(s32[16,2,1]{1,2,0:T(1,128)} %bitcast.1), calls=%async_computation | async-start | bytes 16384 | tf_op jit(solution)/shard_map/all_to_all | solution.py:94
  26.1 1.5 copy.21
  28.1 1.0 copy.22
  29.1 1.6 convolution_convert_fusion.1
  30.7 1.5 all_to_all.21
  32.2 11.1 %all-to-all-done = s32[16,2,1]{1,2,0:T(1,128)S(1)} async-done(((s32[16,2,1]{1,2,0:T(1,128)}), s32[16,2,1]{1,2,0:T(1,128)S(1)}, u32[]{:S(2)}, u32[]{:S(2)}) %all-to-all-start) | async-done | bytes 160 | tf_op jit(solution)/shard_map/all_to_all | solution.py:94
  43.3 5.8 all-to-all-start.1
  49.1 0.5 broadcast.187
  49.7 0.7 reduce.4
  50.4 44.3 %all-to-all-done.1 = bf16[16,2,16384]{2,1,0:T(2,128)(2,1)S(1)} async-done(((bf16[16,2,16384]{2,1,0:T(2,128)(2,1)}), bf16[16,2,16384]{2,1,0:T(2,128)(2,1)S(1)}, u32[]{:S(2)}, u32[]{:S(2)}) %all-to-all-start.1) | async-done | bytes 1048608 | tf_op jit(solution)/shard_map/all_to_all | solution.py:93
  94.7 1.2 all_to_all.23
  95.9 2.1 multiply_reduce_fusion
  98.1 0.6 fusion.47
  98.7 152.9 %all-reduce.2 = (f32[]{:T(128)}, f32[]{:T(128)}) all-reduce(f32[]{:T(128)} %get-tuple-element.4, f32[]{:T(128)} %fusion.47), channel_id=1, replica_groups=mesh['layer'=8,'row'=8,'col'=16] {'layer','row','col'}, use_global_device_ids=true, to_apply=%region_6.7 | all-reduce | flops 2 | bytes 16 | tf_op jit(solution)/shard_map/psum | solution.py:109
  254.6 1.9 collective-permute-start
  256.5 6.8 %collective-permute-start.1 = (bf16[128,1024]{1,0:T(8,128)(2,1)S(1)}, bf16[128,1024]{1,0:T(8,128)(2,1)}, u32[]{:S(2)}, u32[]{:S(2)}) collective-permute-start(bf16[128,1024]{1,0:T(8,128)(2,1)S(1)} %multiply_convert_fusion.2), channel_id=1, source_target_pairs={{0,3},{1,4},{2,5},{3,6},{4,7},{5,8},{6,9},{7,10},{8,11},{9,12},{10... | collective-permute-start | bytes 786440 | tf_op jit(solution)/shard_map/ppermute | solution.py:10
  263.4 6.3 %collective-permute-start.2 = (bf16[128,1024]{1,0:T(8,128)(2,1)S(1)}, bf16[128,1024]{1,0:T(8,128)(2,1)}, u32[]{:S(2)}, u32[]{:S(2)}) collective-permute-start(bf16[128,1024]{1,0:T(8,128)(2,1)S(1)} %multiply_convert_fusion.2), channel_id=1, source_target_pairs={{0,2},{1,3},{2,4},{3,5},{4,6},{5,7},{6,8},{7,9},{8,10},{9,11},{10,... | collective-permute-start | bytes 786440 | tf_op jit(solution)/shard_map/ppermute | solution.py:10
  269.8 6.9 %collective-permute-start.3 = (bf16[128,1024]{1,0:T(8,128)(2,1)S(1)}, bf16[128,1024]{1,0:T(8,128)(2,1)}, u32[]{:S(2)}, u32[]{:S(2)}) collective-permute-start(bf16[128,1024]{1,0:T(8,128)(2,1)S(1)} %multiply_convert_fusion.2), channel_id=1, source_target_pairs={{0,1},{1,2},{2,3},{3,4},{4,5},{5,6},{6,7},{7,8},{8,9},{9,10},{10,1... | collective-permute-start | bytes 786440 | tf_op jit(solution)/shard_map/ppermute | solution.py:10
  276.7 8.8 %collective-permute-start.4 = (bf16[128,1024]{1,0:T(8,128)(2,1)S(1)}, bf16[128,1024]{1,0:T(8,128)(2,1)}, u32[]{:S(2)}, u32[]{:S(2)}) collective-permute-start(bf16[128,1024]{1,0:T(8,128)(2,1)S(1)} %multiply_convert_fusion.2), channel_id=1, source_target_pairs={{1,0},{2,1},{3,2},{4,3},{5,4},{6,5},{7,6},{8,7},{9,8},{10,9},{11,1... | collective-permute-start | bytes 786440 | tf_op jit(solution)/shard_map/ppermute | solution.py:10
  285.7 1.9 collective-permute-start.5
  287.6 1.0 bitcast_dynamic-update-slice_fusion.14
  288.6 10.7 %collective-permute-done.1 = bf16[128,1024]{1,0:T(8,128)(2,1)} collective-permute-done((bf16[128,1024]{1,0:T(8,128)(2,1)S(1)}, bf16[128,1024]{1,0:T(8,128)(2,1)}, u32[]{:S(2)}, u32[]{:S(2)}) %collective-permute-start.1) | collective-permute-done | bytes 262176 | tf_op jit(solution)/shard_map/ppermute | solution.py:10
  299.3 8.7 %collective-permute-start.6 = (bf16[128,1024]{1,0:T(8,128)(2,1)S(1)}, bf16[128,1024]{1,0:T(8,128)(2,1)S(1)}, u32[]{:S(2)}, u32[]{:S(2)}) collective-permute-start(bf16[128,1024]{1,0:T(8,128)(2,1)S(1)} %multiply_convert_fusion.2), channel_id=1, source_target_pairs={{3,0},{4,1},{5,2},{6,3},{7,4},{8,5},{9,6},{10,7},{11,8},{12,9},{13... | collective-permute-start | bytes 786440 | tf_op jit(solution)/shard_map/ppermute | solution.py:10
  308.0 1.0 bitcast_dynamic-update-slice_fusion.13
  309.0 1.0 bitcast_dynamic-update-slice_fusion.12
  310.0 17.7 %collective-permute-done.3 = bf16[128,1024]{1,0:T(8,128)(2,1)} collective-permute-done((bf16[128,1024]{1,0:T(8,128)(2,1)S(1)}, bf16[128,1024]{1,0:T(8,128)(2,1)}, u32[]{:S(2)}, u32[]{:S(2)}) %collective-permute-start.3) | collective-permute-done | bytes 262176 | tf_op jit(solution)/shard_map/ppermute | solution.py:10
  327.7 1.0 bitcast_dynamic-update-slice_fusion.11
  328.8 34.2 %collective-permute-done.4 = bf16[128,1024]{1,0:T(8,128)(2,1)} collective-permute-done((bf16[128,1024]{1,0:T(8,128)(2,1)S(1)}, bf16[128,1024]{1,0:T(8,128)(2,1)}, u32[]{:S(2)}, u32[]{:S(2)}) %collective-permute-start.4) | collective-permute-done | bytes 262176 | tf_op jit(solution)/shard_map/ppermute | solution.py:10
  363.0 1.0 bitcast_dynamic-update-slice_fusion.10
  364.9 1.9 collective-permute-start.7
  366.9 5.7 collective-permute-start.8
  372.6 1.9 collective-permute-start.9
  374.5 47.5 %collective-permute-start.10 = (bf16[128,1024]{1,0:T(8,128)(2,1)S(1)}, bf16[128,1024]{1,0:T(8,128)(2,1)S(1)}, u32[]{:S(2)}, u32[]{:S(2)}) collective-permute-start(bf16[128,1024]{1,0:T(8,128)(2,1)S(1)} %fusion.7), channel_id=1, source_target_pairs={{0,1},{1,2},{2,3},{3,4},{4,5},{5,6},{6,7},{7,8},{8,9},{9,10},{10,1... | collective-permute-start | bytes 786440 | tf_op jit(solution)/shard_map/ppermute | solution.py:10
  422.0 1.9 collective-permute-start.11
  423.9 1.9 collective-permute-start.12
  425.8 0.7 collective-permute-done.8
  426.5 1.9 collective-permute-start.13
  428.5 3.7 collective-permute-done.10
  432.2 9.7 %collective-permute-done.11 = bf16[128,1024]{1,0:T(8,128)(2,1)S(1)} collective-permute-done((bf16[128,1024]{1,0:T(8,128)(2,1)S(1)}, bf16[128,1024]{1,0:T(8,128)(2,1)S(1)}, u32[]{:S(2)}, u32[]{:S(2)}) %collective-permute-start.11) | collective-permute-done | bytes 262176 | tf_op jit(solution)/shard_map/ppermute | solution.py:10
  442.0 79.3 %collective-permute-done.13 = bf16[128,1024]{1,0:T(8,128)(2,1)S(1)} collective-permute-done((bf16[128,1024]{1,0:T(8,128)(2,1)S(1)}, bf16[128,1024]{1,0:T(8,128)(2,1)S(1)}, u32[]{:S(2)}, u32[]{:S(2)}) %collective-permute-start.13) | collective-permute-done | bytes 262176 | tf_op jit(solution)/shard_map/ppermute | solution.py:10
  522.6 1.5 all_to_all.24
  524.1 93.4 %all_to_all.30 = bf16[16,2,16384]{2,1,0:T(2,128)(2,1)} all-to-all(bf16[16,2,16384]{2,1,0:T(2,128)(2,1)} %all_to_all.24), channel_id=1, replica_groups=mesh['layer'=8,'row'=8,'col'=16] {'col'}, dimensions={0} | all-to-all | bytes 2097152 | tf_op jit(solution)/shard_map/all_to_all | solution.py:140
  617.4 1.5 all_to_all.26
  619.4 1.1 fusion.1
  (63 shorter events, 3.9 us)
Async XLA Ops:
  0.6 27.0 %copy-start = (bf16[16,256,128]{2,1,0:T(8,128)(2,1)S(1)}, bf16[16,256,128]{2,1,0:T(8,128)(2,1)}, u32[]{:S(2)}) copy-start(bf16[16,256,128]{2,1,0:T(8,128)(2,1)} %param.7) | copy-start | bytes 3145732
  0.6 27.0 %copy-start.2 = (f32[16,256]{1,0:T(8,128)S(1)}, f32[16,256]{1,0:T(8,128)}, u32[]{:S(2)}) copy-start(f32[16,256]{1,0:T(8,128)} %param.9) | copy-start | bytes 49156
  3.8 39.5 %all-to-all-start = ((s32[16,2,1]{1,2,0:T(1,128)}), s32[16,2,1]{1,2,0:T(1,128)S(1)}, u32[]{:S(2)}, u32[]{:S(2)}) async-start(s32[16,2,1]{1,2,0:T(1,128)} %bitcast.1), calls=%async_computation | async-start | bytes 16384 | tf_op jit(solution)/shard_map/all_to_all | solution.py:94
  30.7 18.4 %copy-start.3 = (s32[1,8]{1,0:T(1,128)S(1)}, s32[1,8]{1,0:T(1,128)}, u32[]{:S(2)}) copy-start(s32[1,8]{1,0:T(1,128)} %param.12) | copy-start | bytes 100
  43.3 51.5 %all-to-all-start.1 = ((bf16[16,2,16384]{2,1,0:T(2,128)(2,1)}), bf16[16,2,16384]{2,1,0:T(2,128)(2,1)S(1)}, u32[]{:S(2)}, u32[]{:S(2)}) async-start(bf16[16,2,16384]{2,1,0:T(2,128)(2,1)} %all_to_all.21), calls=%async_computation.1 | async-start | bytes 2097152 | tf_op jit(solution)/shard_map/all_to_all | solution.py:93
  95.9 160.6 %copy-start.4 = (s32[1,8]{1,0:T(1,128)S(1)}, s32[1,8]{1,0:T(1,128)}, u32[]{:S(2)}) copy-start(s32[1,8]{1,0:T(1,128)} %param.13) | copy-start | bytes 100
  254.6 31.1 %collective-permute-start = (bf16[128,1024]{1,0:T(8,128)(2,1)S(1)}, bf16[128,1024]{1,0:T(8,128)(2,1)}, u32[]{:S(2)}, u32[]{:S(2)}) collective-permute-start(bf16[128,1024]{1,0:T(8,128)(2,1)S(1)} %multiply_convert_fusion.2), channel_id=1, source_target_pairs={{0,4},{1,5},{2,6},{3,7},{4,8},{5,9},{6,10},{7,11},{8,12},{9,13},{1... | collective-permute-start | bytes 786440 | tf_op jit(solution)/shard_map/ppermute | solution.py:10
  256.5 42.8 %collective-permute-start.1 = (bf16[128,1024]{1,0:T(8,128)(2,1)S(1)}, bf16[128,1024]{1,0:T(8,128)(2,1)}, u32[]{:S(2)}, u32[]{:S(2)}) collective-permute-start(bf16[128,1024]{1,0:T(8,128)(2,1)S(1)} %multiply_convert_fusion.2), channel_id=1, source_target_pairs={{0,3},{1,4},{2,5},{3,6},{4,7},{5,8},{6,9},{7,10},{8,11},{9,12},{10... | collective-permute-start | bytes 786440 | tf_op jit(solution)/shard_map/ppermute | solution.py:10
  263.4 45.6 %collective-permute-start.2 = (bf16[128,1024]{1,0:T(8,128)(2,1)S(1)}, bf16[128,1024]{1,0:T(8,128)(2,1)}, u32[]{:S(2)}, u32[]{:S(2)}) collective-permute-start(bf16[128,1024]{1,0:T(8,128)(2,1)S(1)} %multiply_convert_fusion.2), channel_id=1, source_target_pairs={{0,2},{1,3},{2,4},{3,5},{4,6},{5,7},{6,8},{7,9},{8,10},{9,11},{10,... | collective-permute-start | bytes 786440 | tf_op jit(solution)/shard_map/ppermute | solution.py:10
  269.8 57.9 %collective-permute-start.3 = (bf16[128,1024]{1,0:T(8,128)(2,1)S(1)}, bf16[128,1024]{1,0:T(8,128)(2,1)}, u32[]{:S(2)}, u32[]{:S(2)}) collective-permute-start(bf16[128,1024]{1,0:T(8,128)(2,1)S(1)} %multiply_convert_fusion.2), channel_id=1, source_target_pairs={{0,1},{1,2},{2,3},{3,4},{4,5},{5,6},{6,7},{7,8},{8,9},{9,10},{10,1... | collective-permute-start | bytes 786440 | tf_op jit(solution)/shard_map/ppermute | solution.py:10
  276.7 86.3 %collective-permute-start.4 = (bf16[128,1024]{1,0:T(8,128)(2,1)S(1)}, bf16[128,1024]{1,0:T(8,128)(2,1)}, u32[]{:S(2)}, u32[]{:S(2)}) collective-permute-start(bf16[128,1024]{1,0:T(8,128)(2,1)S(1)} %multiply_convert_fusion.2), channel_id=1, source_target_pairs={{1,0},{2,1},{3,2},{4,3},{5,4},{6,5},{7,6},{8,7},{9,8},{10,9},{11,1... | collective-permute-start | bytes 786440 | tf_op jit(solution)/shard_map/ppermute | solution.py:10
  285.7 78.3 %collective-permute-start.5 = (bf16[128,1024]{1,0:T(8,128)(2,1)S(1)}, bf16[128,1024]{1,0:T(8,128)(2,1)S(1)}, u32[]{:S(2)}, u32[]{:S(2)}) collective-permute-start(bf16[128,1024]{1,0:T(8,128)(2,1)S(1)} %multiply_convert_fusion.2), channel_id=1, source_target_pairs={{2,0},{3,1},{4,2},{5,3},{6,4},{7,5},{8,6},{9,7},{10,8},{11,9},{12,... | collective-permute-start | bytes 786440 | tf_op jit(solution)/shard_map/ppermute | solution.py:10
  299.3 64.7 %collective-permute-start.6 = (bf16[128,1024]{1,0:T(8,128)(2,1)S(1)}, bf16[128,1024]{1,0:T(8,128)(2,1)S(1)}, u32[]{:S(2)}, u32[]{:S(2)}) collective-permute-start(bf16[128,1024]{1,0:T(8,128)(2,1)S(1)} %multiply_convert_fusion.2), channel_id=1, source_target_pairs={{3,0},{4,1},{5,2},{6,3},{7,4},{8,5},{9,6},{10,7},{11,8},{12,9},{13... | collective-permute-start | bytes 786440 | tf_op jit(solution)/shard_map/ppermute | solution.py:10
  364.9 59.0 %collective-permute-start.7 = (bf16[128,1024]{1,0:T(8,128)(2,1)S(1)}, bf16[128,1024]{1,0:T(8,128)(2,1)S(1)}, u32[]{:S(2)}, u32[]{:S(2)}) collective-permute-start(bf16[128,1024]{1,0:T(8,128)(2,1)S(1)} %fusion.7), channel_id=1, source_target_pairs={{0,4},{1,5},{2,6},{3,7},{4,8},{5,9},{6,10},{7,11},{8,12},{9,13},{1... | collective-permute-start | bytes 786440 | tf_op jit(solution)/shard_map/ppermute | solution.py:10
  366.9 59.7 %collective-permute-start.8 = (bf16[128,1024]{1,0:T(8,128)(2,1)S(1)}, bf16[128,1024]{1,0:T(8,128)(2,1)S(1)}, u32[]{:S(2)}, u32[]{:S(2)}) collective-permute-start(bf16[128,1024]{1,0:T(8,128)(2,1)S(1)} %fusion.7), channel_id=1, source_target_pairs={{0,3},{1,4},{2,5},{3,6},{4,7},{5,8},{6,9},{7,10},{8,11},{9,12},{10... | collective-permute-start | bytes 786440 | tf_op jit(solution)/shard_map/ppermute | solution.py:10
  372.6 55.9 %collective-permute-start.9 = (bf16[128,1024]{1,0:T(8,128)(2,1)S(1)}, bf16[128,1024]{1,0:T(8,128)(2,1)S(1)}, u32[]{:S(2)}, u32[]{:S(2)}) collective-permute-start(bf16[128,1024]{1,0:T(8,128)(2,1)S(1)} %fusion.7), channel_id=1, source_target_pairs={{0,2},{1,3},{2,4},{3,5},{4,6},{5,7},{6,8},{7,9},{8,10},{9,11},{10,... | collective-permute-start | bytes 786440 | tf_op jit(solution)/shard_map/ppermute | solution.py:10
  374.5 57.7 %collective-permute-start.10 = (bf16[128,1024]{1,0:T(8,128)(2,1)S(1)}, bf16[128,1024]{1,0:T(8,128)(2,1)S(1)}, u32[]{:S(2)}, u32[]{:S(2)}) collective-permute-start(bf16[128,1024]{1,0:T(8,128)(2,1)S(1)} %fusion.7), channel_id=1, source_target_pairs={{0,1},{1,2},{2,3},{3,4},{4,5},{5,6},{6,7},{7,8},{8,9},{9,10},{10,1... | collective-permute-start | bytes 786440 | tf_op jit(solution)/shard_map/ppermute | solution.py:10
  422.0 20.0 %collective-permute-start.11 = (bf16[128,1024]{1,0:T(8,128)(2,1)S(1)}, bf16[128,1024]{1,0:T(8,128)(2,1)S(1)}, u32[]{:S(2)}, u32[]{:S(2)}) collective-permute-start(bf16[128,1024]{1,0:T(8,128)(2,1)S(1)} %fusion.7), channel_id=1, source_target_pairs={{1,0},{2,1},{3,2},{4,3},{5,4},{6,5},{7,6},{8,7},{9,8},{10,9},{11,1... | collective-permute-start | bytes 786440 | tf_op jit(solution)/shard_map/ppermute | solution.py:10
  423.9 18.1 %collective-permute-start.12 = (bf16[128,1024]{1,0:T(8,128)(2,1)S(1)}, bf16[128,1024]{1,0:T(8,128)(2,1)S(1)}, u32[]{:S(2)}, u32[]{:S(2)}) collective-permute-start(bf16[128,1024]{1,0:T(8,128)(2,1)S(1)} %fusion.7), channel_id=1, source_target_pairs={{2,0},{3,1},{4,2},{5,3},{6,4},{7,5},{8,6},{9,7},{10,8},{11,9},{12,... | collective-permute-start | bytes 786440 | tf_op jit(solution)/shard_map/ppermute | solution.py:10
  426.5 94.8 %collective-permute-start.13 = (bf16[128,1024]{1,0:T(8,128)(2,1)S(1)}, bf16[128,1024]{1,0:T(8,128)(2,1)S(1)}, u32[]{:S(2)}, u32[]{:S(2)}) collective-permute-start(bf16[128,1024]{1,0:T(8,128)(2,1)S(1)} %fusion.7), channel_id=1, source_target_pairs={{3,0},{4,1},{5,2},{6,3},{7,4},{8,5},{9,6},{10,7},{11,8},{12,9},{13... | collective-permute-start | bytes 786440 | tf_op jit(solution)/shard_map/ppermute | solution.py:10
  522.0 95.4 %copy-start.1 = (bf16[128,1024]{1,0:T(8,128)(2,1)}, bf16[128,1024]{1,0:T(8,128)(2,1)S(1)}, u32[]{:S(2)}) copy-start(bf16[128,1024]{1,0:T(8,128)(2,1)S(1)} %fusion.6) | copy-start | bytes 786436
where the time goes:
time: 622 us; the launch traced here: 621 us
  blocking collectives  246 us (40%)
  waiting for transfers between devices  211 us (34%)
  starting transfers between devices  132 us (21%)
  local copies, waits for them, and re-layouts  15.2 us (2%)
  matrix products  7.01 us (1%)
    ppermute x14, waiting for transfers between devices, passed_along(): lax.ppermute(value, axis, [(source, source + steps) for source in range(f...  156 us
    psum x1, blocking collectives, shards(): lax.psum((trace_part, square_part), ('layer', 'row', 'col'))  153 us
    ppermute x14, starting transfers between devices, passed_along(): lax.ppermute(value, axis, [(source, source + steps) for source in range(f...  104 us
    all_to_all x1, blocking collectives, shards(): lax.all_to_all(answers, 'col', split_axis=0, concat_axis=0, tiled=True)  93.4 us
    all_to_all x1, waiting for transfers between devices, shards(): lax.all_to_all(outgoing, 'col', split_axis=0, concat_axis=0, tiled=True)  44.3 us
    all_to_all x1, starting transfers between devices, shards(): lax.all_to_all(labels, 'col', split_axis=0, concat_axis=0, tiled=True)  22.3 us
  transfers between devices with their start and end apart: 16, of which 9 were waited for; matrix products, arithmetic and copies ran while one was open for 2% of the time, Pallas kernels for 0%

commit v1 on v0

v1 whole, which is shorter than its diff:
```python
import functools

import jax
import jax.numpy as jnp
from jax import lax
from jax.experimental import pallas as pl
from jax.experimental.pallas import tpu as pltpu
from jax.sharding import Mesh, PartitionSpec as P

BW = 128
SLOTS = 8
HALF = 4
META = 16
WIDE = 9 * BW
LINE = ("layer", "row", "ring")
F32 = jnp.float32
BF16 = jnp.bfloat16
VMEM = pl.BlockSpec(memory_space=pltpu.VMEM)
SMEM = pl.BlockSpec(memory_space=pltpu.SMEM)

REACH = {
    -1: [(-2, s) for s in range(2, 8)] + [(-1, s) for s in range(1, 8)],
    -2: [(-4, s) for s in range(4, 8)] + [(-3, s) for s in range(3, 8)],
    1: [(2, s) for s in range(0, 7)] + [(3, s) for s in range(0, 6)],
    2: [(4, s) for s in range(0, 5)],
}
SIDES = (-1, -2, 1, 2)
OWN = [(r, s) for r in range(2) for s in range(SLOTS)]


def call(kernel, out_shape, in_specs, out_specs, scratch=(), flops=0, moved=0):
    return pl.pallas_call(
        kernel,
        out_shape=out_shape,
        in_specs=in_specs,
        out_specs=out_specs,
        scratch_shapes=list(scratch),
        compiler_params=pltpu.CompilerParams(vmem_limit_bytes=24 * 1024 * 1024),
        cost_estimate=pl.CostEstimate(flops=flops, bytes_accessed=moved, transcendentals=0),
    )


def rows(block):
    return slice(block * BW, (block + 1) * BW)


def integrate(route, slot, w, prow, pcol, out, pos_out, count):
    batches, points, _ = prow.shape
    dests, depth, _ = out.shape
    for t in range(2 * dests):
        count[t] = 0
    w_cols = jnp.concatenate([w[...], jnp.zeros((BW - batches, points), F32)], axis=0).T
    line = lax.broadcasted_iota(jnp.int32, (dests * META, BW), 0)
    named = jnp.where(line % META < 4, line // META * 4 + line % META, -1)
    labels = jnp.zeros((dests * META, BW), F32)
    for b in range(batches):
        t = route[b, 0]
        rank = count[t]
        count[t] = rank + 1
        pos = t * 2 + jnp.minimum(rank, 1)
        pos_out[b] = pos
        labels = jnp.where(named == pos, (slot[b] + 1).astype(F32), labels)
        scaled = (w_cols[:, b : b + 1] * pcol[b].astype(F32)).astype(BF16)
        made = lax.dot_general(
            prow[b], scaled, (((0,), (0,)), ((), ())), preferred_element_type=F32
        )
        at = pl.multiple_of(pos % 4 * BW, BW)
        out[pos // 4, pl.ds(at, BW), :] = (made / points).astype(BF16)
    for d in range(dests):
        out[d, 4 * BW : 4 * BW + META, :] = labels[d * META : (d + 1) * META].astype(BF16)


def accumulate(labels, arrived, ham, dens, out, total):
    total[...] = jnp.zeros_like(total)
    for i in range(4 * arrived.shape[0]):
        label = labels[i]

        @pl.when(label > 0)
        def _():
            at = (i % 4 // 2) * SLOTS + label - 1
            total[at] += arrived[i // 4, rows(i % 4), :].astype(F32)

    for k in range(2 * SLOTS):
        out[rows(k), :] = total[k].astype(BF16)
    line = lax.broadcasted_iota(jnp.int32, (META, BW), 0)
    meta = jnp.zeros((META, BW), F32)
    for s in range(SLOTS):
        meta = jnp.where(line == s, ham[0, s].astype(F32), meta)
        meta = jnp.where(line == s + SLOTS, dens[0, s].astype(F32), meta)
    out[2 * SLOTS * BW :, :] = meta.astype(BF16)


def combine(place, own, other, ham, p1, p2, m1, m2, sums, *, pairs):
    side, pair = place[0], place[1]
    tail = slice(2 * SLOTS * BW, 2 * SLOTS * BW + META)
    meta_own, meta_other = own[tail, :].astype(F32), other[tail, :].astype(F32)
    line = lax.broadcasted_iota(jnp.int32, (SLOTS, BW), 0)
    square = jnp.zeros((BW, BW), F32)
    diag = jnp.zeros((BW, BW), F32)
    masks = []
    for r in range(2):
        mine = side == r
        usable = jnp.where(mine, meta_own[:SLOTS], meta_other[:SLOTS])
        masks.append(jnp.where(mine, meta_own[SLOTS:], meta_other[SLOTS:]))
        column = 2 * pair + r + line - HALF
        usable = jnp.where((column >= 0) & (column < 2 * pairs), usable, 0.0)
        for s in range(SLOTS):
            k = r * SLOTS + s
            value = own[rows(k), :].astype(F32) + other[rows(k), :].astype(F32)
            block = (value * usable[s : s + 1, :]).astype(BF16)
            ham[rows(k), :] = block
            wide = block.astype(F32)
            square += wide * wide
            if s == HALF:
                diag += wide
    eye = lax.broadcasted_iota(jnp.int32, (BW, BW), 0) == lax.broadcasted_iota(
        jnp.int32, (BW, BW), 1
    )
    trace_sum = jnp.sum(jnp.where(eye, diag, 0.0), axis=(0, 1), keepdims=True)
    square_sum = jnp.sum(square, axis=(0, 1), keepdims=True)
    sums[...] = jnp.where(line == 0, trace_sum, square_sum)
    meta = jnp.concatenate(masks, axis=0).astype(BF16)
    ham[tail, :] = meta
    for piece, towards in ((p1, 1), (p2, 2), (m1, -1), (m2, -2)):
        send_piece(ham, piece, towards)
        piece[len(REACH[-towards]) * BW :, :] = meta


def send_piece(source, piece, towards):
    for i, (b, s) in enumerate(REACH[-towards]):
        r = b + 2 * towards
        piece[rows(i), :] = source[rows(r * SLOTS + s), :]


def fill(right, ours, near, make):
    places = [(ours, i, b, s) for i, (b, s) in enumerate(OWN)]
    for piece, which in zip(near, SIDES):
        places += [(piece, i, b, s) for i, (b, s) in enumerate(REACH[which])]
    given = set()
    for piece, i, b, s in places:
        c = b + s - HALF
        given.add((b, c))
        right[rows(b + HALF), rows(c + HALF)] = make(piece, i, b, s)
    for b in range(-HALF, HALF + 1):
        for c in range(-HALF, HALF + 1):
            if (b, c) not in given:
                right[rows(b + HALF), rows(c + HALF)] = jnp.zeros((BW, BW), BF16)


def square_pair(right):
    left = right[HALF * BW : (HALF + 2) * BW, :]
    for j in range(3):
        span = slice(j * 3 * BW, (j + 1) * 3 * BW)
        yield j, jnp.dot(left, right[:, span], preferred_element_type=F32)


def first_square(ham, a1, a2, b1, b2, out, p1, p2, m1, m2, right):
    fill(right, ham, (a1, a2, b1, b2), lambda piece, i, b, s: piece[rows(i), :])
    for j, made in square_pair(right):
        for i in range(3):
            for r in range(2):
                s = 3 * j + i - r
                if 0 <= s < SLOTS:
                    out[rows(r * SLOTS + s), :] = made[rows(r), rows(i)].astype(BF16)
    for piece, towards in ((p1, 1), (p2, 2), (m1, -1), (m2, -2)):
        send_piece(out, piece, towards)


def second_square(
    place, labels, sums, ham, ha1, ha2, hb1, hb2, sq, ga1, ga2, gb1, gb2,
    density, answers, right, blocks, *, order,
):
    side = place[0]
    average = sums[0:1, :] / order
    spread = jnp.sqrt(sums[1:2, :] / order - average * average + 1e-06)
    lift = 0.5 + average / (4.0 * spread)
    scaling = 1.0 / (4.0 * spread)
    unit, linear, quadratic = lift * lift, 2.0 * lift * scaling, scaling * scaling
    eye = lax.broadcasted_iota(jnp.int32, (BW, BW), 0) == lax.broadcasted_iota(
        jnp.int32, (BW, BW), 1
    )
    unit_block = jnp.where(eye, jnp.broadcast_to(unit, (BW, BW)), 0.0)
    squares = {id(ham): sq, id(ha1): ga1, id(ha2): ga2, id(hb1): gb1, id(hb2): gb2}
    masks = {}
    for piece in (ham, ha1, ha2, hb1, hb2):
        masks[id(piece)] = piece[piece.shape[0] - META :, :].astype(F32)

    def make(piece, i, b, s):
        line = b % 2 * SLOTS + s
        value = quadratic * squares[id(piece)][rows(i), :].astype(F32)
        value = value - linear * piece[rows(i), :].astype(F32)
        if s == HALF:
            value = value + unit_block
        return (value * masks[id(piece)][line : line + 1, :]).astype(BF16)

    fill(right, ham, (ha1, ha2, hb1, hb2), make)
    mask = masks[id(ham)]
    for j, made in square_pair(right):
        for i in range(3):
            for r in range(2):
                s = 3 * j + i - r
                if 0 <= s < SLOTS:
                    k = r * SLOTS + s
                    first = right[rows(HALF + r), rows(3 * j + i)].astype(F32)
                    value = (2.0 * first - made[rows(r), rows(i)]) * mask[k : k + 1, :]
                    blocks[k] = value.astype(BF16)
    for s in range(SLOTS):
        density[:, rows(s)] = blocks[side * SLOTS + s]
    for i in range(4 * answers.shape[0]):
        label = jnp.maximum(labels[i], 1)
        answers[i // 4, rows(i % 4), :] = blocks[(i % 4 // 2) * SLOTS + label - 1]


def on_grid(pos, returned, prow, pcol, out):
    batches, points, _ = prow.shape
    lane = lax.broadcasted_iota(jnp.int32, (points, BW), 1)
    values = jnp.zeros((points, BW), F32)
    for b in range(batches):
        at = pl.multiple_of(pos[b] % 4 * BW, BW)
        block = returned[pos[b] // 4, pl.ds(at, BW), :]
        partial = jnp.dot(prow[b], block, preferred_element_type=F32) * pcol[b].astype(F32)
        values = jnp.where(lane == b, jnp.sum(partial, axis=1, keepdims=True), values)
    out[...] = values.T[:batches, :]


def moved_along(piece, steps):
    count = lax.axis_size(LINE)
    first, last = max(0, -steps), min(count, count - steps)
    return lax.ppermute(piece, LINE, [(i, i + steps) for i in range(first, last)])


def summed_over_pairs(sums):
    for axis in ("ring", "row", "layer"):
        size = lax.axis_size(axis)
        step = 1
        while step < size:
            sums = sums + lax.ppermute(sums, axis, [(i, i ^ step) for i in range(size)])
            step *= 2
    return sums


def shards(phi_row, phi_col, weights, batch_route, batch_slot, ham_pattern, dens_pattern):
    batches, points, _ = phi_row.shape
    dests = lax.axis_size("ring")
    pairs = lax.axis_size(LINE)
    place = jnp.stack([lax.axis_index("side"), lax.axis_index(LINE)]).astype(jnp.int32)
    depth = 4 * BW + META

    def shape(*dims, kind=BF16):
        return jax.ShapeDtypeStruct(dims, kind)

    outgoing, position = call(
        integrate,
        (shape(dests, depth, BW), shape(batches, kind=jnp.int32)),
        [SMEM, SMEM, VMEM, VMEM, VMEM],
        (VMEM, SMEM),
        [pltpu.SMEM((2 * dests,), jnp.int32)],
        flops=2 * batches * points * BW * BW,
        moved=6 << 20,
    )(batch_route, batch_slot, weights, phi_row, phi_col)
    arrived = lax.all_to_all(outgoing, "ring", split_axis=0, concat_axis=0, tiled=True)
    labels = arrived[:, 4 * BW : 4 * BW + 4, 0].astype(jnp.int32).reshape(4 * dests)

    whole = 2 * SLOTS * BW + META
    part = call(
        accumulate,
        shape(whole, BW),
        [SMEM, VMEM, SMEM, SMEM],
        VMEM,
        [pltpu.VMEM((2 * SLOTS, BW, BW), F32)],
        moved=4 << 20,
    )(labels, arrived, ham_pattern, dens_pattern)
    other = lax.ppermute(part, "side", [(0, 1), (1, 0)])

    size = {t: len(REACH[-t]) * BW for t in (1, 2, -1, -2)}
    ham, p1, p2, m1, m2, sums = call(
        functools.partial(combine, pairs=pairs),
        (shape(whole, BW),)
        + tuple(shape(size[t] + META, BW) for t in (1, 2, -1, -2))
        + (shape(SLOTS, BW, kind=F32),),
        [SMEM, VMEM, VMEM],
        (VMEM,) * 6,
        moved=4 << 20,
    )(place, part, other)
    near = [moved_along(p, t) for p, t in ((p1, 1), (p2, 2), (m1, -1), (m2, -2))]
    sums = summed_over_pairs(sums)

    sq, p1, p2, m1, m2 = call(
        first_square,
        (shape(2 * SLOTS * BW, BW),) + tuple(shape(size[t], BW) for t in (1, 2, -1, -2)),
        [VMEM] * 5,
        (VMEM,) * 5,
        [pltpu.VMEM((WIDE, WIDE), BF16)],
        flops=4 * BW * WIDE * WIDE,
        moved=4 << 20,
    )(ham, *near)
    near_sq = [moved_along(p, t) for p, t in ((p1, 1), (p2, 2), (m1, -1), (m2, -2))]

    density, answers = call(
        functools.partial(second_square, order=2 * pairs * BW),
        (shape(BW, SLOTS * BW), shape(dests, 4 * BW, BW)),
        [SMEM, SMEM] + [VMEM] * 11,
        (VMEM, VMEM),
        [pltpu.VMEM((WIDE, WIDE), BF16), pltpu.VMEM((2 * SLOTS, BW, BW), BF16)],
        flops=4 * BW * WIDE * WIDE,
        moved=6 << 20,
    )(place, labels, sums, ham, *near, sq, *near_sq)
    returned = lax.all_to_all(answers, "ring", split_axis=0, concat_axis=0, tiled=True)

    grid_density = call(
        on_grid,
        shape(batches, points, kind=F32),
        [SMEM, VMEM, VMEM, VMEM],
        VMEM,
        flops=2 * batches * points * BW * BW,
        moved=6 << 20,
    )(position, returned, phi_row, phi_col)
    return (density, grid_density)


def solution(mesh):
    layer, row, col = (mesh.shape[a] for a in ("layer", "row", "col"))
    split = Mesh(
        mesh.devices.reshape(layer, row, col // 2, 2), ("layer", "row", "ring", "side")
    )
    axes = ("layer", "row", "ring", "side")
    in_specs = (
        P(axes, None, None),
        P(axes, None, None),
        P(axes, None),
        P(axes, None),
        P(axes),
        P(axes, None),
        P(axes, None),
    )
    out_specs = (P(axes, None), P(axes, None))
    return jax.shard_map(
        shards, mesh=split, in_specs=in_specs, out_specs=out_specs, check_vma=False
    )
```

time: 622 us -> 261 us (0.42)
  the two profiles are of different devices: /device:TPU:132 before, /device:TPU:770 now
where the time goes in v1:
time: 261 us
  waiting for transfers between devices  92.1 us (35%)
  starting transfers between devices  85.8 us (33%)
  blocking collectives  65.9 us (25%)
  Pallas kernels  10.9 us (4%)
  local copies, waits for them, and re-layouts  4.65 us (2%)
    ppermute x8, starting transfers between devices, moved_along(): lax.ppermute(piece, LINE, [(i, i + steps) for i in range(first, last)])  66.2 us
    ppermute x1, waiting for transfers between devices, shards(): other = lax.ppermute(part, 'side', [(0, 1), (1, 0)])  43.2 us
    ppermute x9, waiting for transfers between devices, summed_over_pairs(): sums = sums + lax.ppermute(sums, axis, [(i, i ^ step) for i in range(size)])  40.3 us
    all_to_all x1, blocking collectives, shards(): lax.all_to_all(outgoing, 'ring', split_axis=0, concat_axis=0, tiled=True)  36.3 us
    all_to_all x1, blocking collectives, shards(): lax.all_to_all(answers, 'ring', split_axis=0, concat_axis=0, tiled=True)  29.6 us
    ppermute x9, starting transfers between devices, summed_over_pairs(): sums = sums + lax.ppermute(sums, axis, [(i, i ^ step) for i in range(size)])  17.7 us
    ppermute x8, waiting for transfers between devices, moved_along(): lax.ppermute(piece, LINE, [(i, i + steps) for i in range(first, last)])  8.61 us
  transfers between devices with their start and end apart: 18, of which 12 were waited for; matrix products, arithmetic and copies ran while one was open for 0% of the time, Pallas kernels for 0%

profile of v1, /device:TPU:770, one launch (start us, length us, event | category | flops | bytes accessed | tf_op | source)
XLA Modules:
  0.0 260.6 jit_solution(8335922325158615372)
XLA Ops:
  0.6 0.7 copy.10.route
  1.4 1.2 copy-done
  2.6 1.2 copy-done.2
  3.8 0.7 copy-done.4
  4.5 0.7 copy-done.5
  5.2 2.3 shard_map.86
  7.5 0.0 copy-start.6
  7.6 0.0 copy-start.7
  7.6 36.3 %all_to_all.10.arrived = bf16[8,528,128]{2,1,0:T(8,128)(2,1)S(1)} all-to-all(bf16[8,528,128]{2,1,0:T(8,128)(2,1)S(1)} %get-tuple-element.17), channel_id=1, replica_groups=mesh['layer'=8,'row'=8,'ring'=8,'side'=2] {'ring'}, dimensions={0} | all-to-all | bytes 2162688 | tf_op jit(solution)/shard_map/all_to_all | solution.py:261
  43.9 0.2 convert_reduce_fusion
  44.1 0.1 reshape.8.labels
  44.2 1.0 shard_map.87.own
  45.2 1.9 collective-permute-start
  47.1 0.1 pad_add_fusion.place
  47.2 43.2 %collective-permute-done.other = bf16[2064,128]{1,0:T(8,128)(2,1)S(1)} collective-permute-done((bf16[2064,128]{1,0:T(8,128)(2,1)S(1)}, bf16[2064,128]{1,0:T(8,128)(2,1)S(1)}, u32[]{:S(2)}, u32[]{:S(2)}) %collective-permute-start) | collective-permute-done | bytes 528416 | tf_op jit(solution)/shard_map/ppermute | solution.py:273
  90.4 1.0 shard_map.88
  91.4 1.9 collective-permute-start.10
  93.3 35.0 %collective-permute-start.12 = (bf16[1680,128]{1,0:T(8,128)(2,1)S(1)}, bf16[1680,128]{1,0:T(8,128)(2,1)S(1)}, u32[]{:S(2)}, u32[]{:S(2)}) collective-permute-start(bf16[1680,128]{1,0:T(8,128)(2,1)S(1)} %get-tuple-element.22), channel_id=1, source_target_pairs={{2,0},{4,2},{6,4},{8,6},{10,8},{12,10},{14,12},{16,14},{18,16},{20... | collective-permute-start | bytes 1290248 | tf_op jit(solution)/shard_map/ppermute | solution.py:229
  128.3 1.9 collective-permute-start.11
  130.3 8.1 %collective-permute-start.13 = (bf16[656,128]{1,0:T(8,128)(2,1)S(1)}, bf16[656,128]{1,0:T(8,128)(2,1)S(1)}, u32[]{:S(2)}, u32[]{:S(2)}) collective-permute-start(bf16[656,128]{1,0:T(8,128)(2,1)S(1)} %get-tuple-element.23), channel_id=1, source_target_pairs={{4,0},{6,2},{8,4},{10,6},{12,8},{14,10},{16,12},{18,14},{20,16},{2... | collective-permute-start | bytes 503816 | tf_op jit(solution)/shard_map/ppermute | solution.py:229
  138.4 4.0 %collective-permute-done.13.b2.hb2 = bf16[656,128]{1,0:T(8,128)(2,1)S(1)} collective-permute-done((bf16[656,128]{1,0:T(8,128)(2,1)S(1)}, bf16[656,128]{1,0:T(8,128)(2,1)S(1)}, u32[]{:S(2)}, u32[]{:S(2)}) %collective-permute-start.13) | collective-permute-done | bytes 167968 | tf_op jit(solution)/shard_map/ppermute | solution.py:229
  142.4 4.6 %collective-permute-done.11.a2.ha2 = bf16[1168,128]{1,0:T(8,128)(2,1)S(1)} collective-permute-done((bf16[1168,128]{1,0:T(8,128)(2,1)S(1)}, bf16[1168,128]{1,0:T(8,128)(2,1)S(1)}, u32[]{:S(2)}, u32[]{:S(2)}) %collective-permute-start.11) | collective-permute-done | bytes 299040 | tf_op jit(solution)/shard_map/ppermute | solution.py:229
  147.0 1.4 shard_map.89
  148.5 2.6 %collective-permute-start.14 = (bf16[1664,128]{1,0:T(8,128)(2,1)S(1)}, bf16[1664,128]{1,0:T(8,128)(2,1)S(1)}, u32[]{:S(2)}, u32[]{:S(2)}) collective-permute-start(bf16[1664,128]{1,0:T(8,128)(2,1)S(1)} %get-tuple-element.25), channel_id=1, source_target_pairs={{0,2},{2,4},{4,6},{6,8},{8,10},{10,12},{12,14},{14,16},{16,18},{18... | collective-permute-start | bytes 1277960 | tf_op jit(solution)/shard_map/ppermute | solution.py:229
  151.1 6.5 %collective-permute-start.16 = (bf16[1664,128]{1,0:T(8,128)(2,1)S(1)}, bf16[1664,128]{1,0:T(8,128)(2,1)S(1)}, u32[]{:S(2)}, u32[]{:S(2)}) collective-permute-start(bf16[1664,128]{1,0:T(8,128)(2,1)S(1)} %get-tuple-element.27), channel_id=1, source_target_pairs={{2,0},{4,2},{6,4},{8,6},{10,8},{12,10},{14,12},{16,14},{18,16},{20... | collective-permute-start | bytes 1277960 | tf_op jit(solution)/shard_map/ppermute | solution.py:229
  157.6 1.9 collective-permute-start.15
  159.6 8.1 %collective-permute-start.17 = (bf16[640,128]{1,0:T(8,128)(2,1)S(1)}, bf16[640,128]{1,0:T(8,128)(2,1)S(1)}, u32[]{:S(2)}, u32[]{:S(2)}) collective-permute-start(bf16[640,128]{1,0:T(8,128)(2,1)S(1)} %get-tuple-element.28), channel_id=1, source_target_pairs={{4,0},{6,2},{8,4},{10,6},{12,8},{14,10},{16,12},{18,14},{20,16},{2... | collective-permute-start | bytes 491528 | tf_op jit(solution)/shard_map/ppermute | solution.py:229
  167.7 1.9 collective-permute-start.1
  169.7 3.6 %collective-permute-done.1 = f32[8,128]{1,0:T(8,128)S(1)} collective-permute-done((f32[8,128]{1,0:T(8,128)S(1)}, f32[8,128]{1,0:T(8,128)S(1)}, u32[]{:S(2)}, u32[]{:S(2)}) %collective-permute-start.1) | collective-permute-done | bytes 4128 | tf_op jit(solution)/shard_map/ppermute | solution.py:237
  173.2 1.9 collective-permute-start.2
  175.1 4.5 %collective-permute-done.2 = f32[8,128]{1,0:T(8,128)S(1)} collective-permute-done((f32[8,128]{1,0:T(8,128)S(1)}, f32[8,128]{1,0:T(8,128)S(1)}, u32[]{:S(2)}, u32[]{:S(2)}) %collective-permute-start.2) | collective-permute-done | bytes 4128 | tf_op jit(solution)/shard_map/ppermute | solution.py:237
  179.6 1.9 collective-permute-start.3
  181.5 7.5 %collective-permute-done.3 = f32[8,128]{1,0:T(8,128)S(1)} collective-permute-done((f32[8,128]{1,0:T(8,128)S(1)}, f32[8,128]{1,0:T(8,128)S(1)}, u32[]{:S(2)}, u32[]{:S(2)}) %collective-permute-start.3) | collective-permute-done | bytes 4128 | tf_op jit(solution)/shard_map/ppermute | solution.py:237
  189.0 1.9 collective-permute-start.4
  190.9 3.6 %collective-permute-done.4 = f32[8,128]{1,0:T(8,128)S(1)} collective-permute-done((f32[8,128]{1,0:T(8,128)S(1)}, f32[8,128]{1,0:T(8,128)S(1)}, u32[]{:S(2)}, u32[]{:S(2)}) %collective-permute-start.4) | collective-permute-done | bytes 4128 | tf_op jit(solution)/shard_map/ppermute | solution.py:237
  194.5 1.9 collective-permute-start.5
  196.4 4.5 %collective-permute-done.5 = f32[8,128]{1,0:T(8,128)S(1)} collective-permute-done((f32[8,128]{1,0:T(8,128)S(1)}, f32[8,128]{1,0:T(8,128)S(1)}, u32[]{:S(2)}, u32[]{:S(2)}) %collective-permute-start.5) | collective-permute-done | bytes 4128 | tf_op jit(solution)/shard_map/ppermute | solution.py:237
  200.9 1.9 collective-permute-start.6
  202.8 7.5 %collective-permute-done.6 = f32[8,128]{1,0:T(8,128)S(1)} collective-permute-done((f32[8,128]{1,0:T(8,128)S(1)}, f32[8,128]{1,0:T(8,128)S(1)}, u32[]{:S(2)}, u32[]{:S(2)}) %collective-permute-start.6) | collective-permute-done | bytes 4128 | tf_op jit(solution)/shard_map/ppermute | solution.py:237
  210.3 1.9 collective-permute-start.7
  212.2 1.1 collective-permute-done.7
  213.4 2.4 collective-permute-start.8
  215.8 3.1 %collective-permute-done.8 = f32[8,128]{1,0:T(8,128)S(1)} collective-permute-done((f32[8,128]{1,0:T(8,128)S(1)}, f32[8,128]{1,0:T(8,128)S(1)}, u32[]{:S(2)}, u32[]{:S(2)}) %collective-permute-start.8) | collective-permute-done | bytes 4128 | tf_op jit(solution)/shard_map/ppermute | solution.py:237
  218.9 1.9 collective-permute-start.9
  220.8 5.1 %collective-permute-done.9 = f32[8,128]{1,0:T(8,128)S(1)} collective-permute-done((f32[8,128]{1,0:T(8,128)S(1)}, f32[8,128]{1,0:T(8,128)S(1)}, u32[]{:S(2)}, u32[]{:S(2)}) %collective-permute-start.9) | collective-permute-done | bytes 4128 | tf_op jit(solution)/shard_map/ppermute | solution.py:237
  225.9 3.2 %shard_map.90 = (bf16[128,1024]{1,0:T(8,128)(2,1)}, bf16[8,512,128]{2,1,0:T(8,128)(2,1)S(1)}) custom-call(s32[2]{0:T(128)S(1)} %pad_add_fusion.place, s32[32]{0:T(128)S(1)} %reshape.8.labels, f32[8,128]{1,0:T(8,128)S(1)} %add.43.sums, bf16[2064,128]{1,0:T(8,128)(2,1)S(1)} %get-tuple-element.19.ham, bf16[1680,128]{1,0:T(8,128)(2,1)S(1)} %collective-permute-done.10.a1.ha1, ...), custom_call_target="tpu_custom_call" | custom-call | flops 679477248 | bytes 6291456 | tf_op jit(solution)/shard_map/pallas_call | solution.py:299
  229.0 29.6 %all_to_all.11.returned = bf16[8,512,128]{2,1,0:T(8,128)(2,1)S(1)} all-to-all(bf16[8,512,128]{2,1,0:T(8,128)(2,1)S(1)} %get-tuple-element.31), channel_id=1, replica_groups=mesh['layer'=8,'row'=8,'ring'=8,'side'=2] {'ring'}, dimensions={0} | all-to-all | bytes 2097152 | tf_op jit(solution)/shard_map/all_to_all | solution.py:308
  258.6 2.0 shard_map.91
  (25 shorter events, 0.1 us)
Async XLA Ops:
  1.4 1.2 copy-start
  2.6 1.2 copy-start.2
  3.8 0.7 copy-start.4
  4.5 0.7 copy-start.5
  7.5 36.6 %copy-start.6 = (s32[1,8]{1,0:T(1,128)S(1)}, s32[1,8]{1,0:T(1,128)}, u32[]{:S(2)}) copy-start(s32[1,8]{1,0:T(1,128)} %ham.1) | copy-start | bytes 100
  7.6 36.6 %copy-start.7 = (s32[1,8]{1,0:T(1,128)S(1)}, s32[1,8]{1,0:T(1,128)}, u32[]{:S(2)}) copy-start(s32[1,8]{1,0:T(1,128)} %dens.1) | copy-start | bytes 100
  45.2 45.2 %collective-permute-start = (bf16[2064,128]{1,0:T(8,128)(2,1)S(1)}, bf16[2064,128]{1,0:T(8,128)(2,1)S(1)}, u32[]{:S(2)}, u32[]{:S(2)}) collective-permute-start(bf16[2064,128]{1,0:T(8,128)(2,1)S(1)} %shard_map.87.own), channel_id=1, source_target_pairs={{0,1},{1,0},{2,3},{3,2},{4,5},{5,4},{6,7},{7,6},{8,9},{9,8},{10,11... | collective-permute-start | bytes 1585160 | tf_op jit(solution)/shard_map/ppermute | solution.py:273
  91.4 55.6 %collective-permute-start.10 = (bf16[1680,128]{1,0:T(8,128)(2,1)S(1)}, bf16[1680,128]{1,0:T(8,128)(2,1)S(1)}, u32[]{:S(2)}, u32[]{:S(2)}) collective-permute-start(bf16[1680,128]{1,0:T(8,128)(2,1)S(1)} %get-tuple-element.20), channel_id=1, source_target_pairs={{0,2},{2,4},{4,6},{6,8},{8,10},{10,12},{12,14},{14,16},{16,18},{18... | collective-permute-start | bytes 1290248 | tf_op jit(solution)/shard_map/ppermute | solution.py:229
  93.3 53.7 %collective-permute-start.12 = (bf16[1680,128]{1,0:T(8,128)(2,1)S(1)}, bf16[1680,128]{1,0:T(8,128)(2,1)S(1)}, u32[]{:S(2)}, u32[]{:S(2)}) collective-permute-start(bf16[1680,128]{1,0:T(8,128)(2,1)S(1)} %get-tuple-element.22), channel_id=1, source_target_pairs={{2,0},{4,2},{6,4},{8,6},{10,8},{12,10},{14,12},{16,14},{18,16},{20... | collective-permute-start | bytes 1290248 | tf_op jit(solution)/shard_map/ppermute | solution.py:229
  128.3 18.7 %collective-permute-start.11 = (bf16[1168,128]{1,0:T(8,128)(2,1)S(1)}, bf16[1168,128]{1,0:T(8,128)(2,1)S(1)}, u32[]{:S(2)}, u32[]{:S(2)}) collective-permute-start(bf16[1168,128]{1,0:T(8,128)(2,1)S(1)} %get-tuple-element.21), channel_id=1, source_target_pairs={{0,4},{2,6},{4,8},{6,10},{8,12},{10,14},{12,16},{14,18},{16,20},{1... | collective-permute-start | bytes 897032 | tf_op jit(solution)/shard_map/ppermute | solution.py:229
  130.3 12.2 %collective-permute-start.13 = (bf16[656,128]{1,0:T(8,128)(2,1)S(1)}, bf16[656,128]{1,0:T(8,128)(2,1)S(1)}, u32[]{:S(2)}, u32[]{:S(2)}) collective-permute-start(bf16[656,128]{1,0:T(8,128)(2,1)S(1)} %get-tuple-element.23), channel_id=1, source_target_pairs={{4,0},{6,2},{8,4},{10,6},{12,8},{14,10},{16,12},{18,14},{20,16},{2... | collective-permute-start | bytes 503816 | tf_op jit(solution)/shard_map/ppermute | solution.py:229
  148.5 77.4 %collective-permute-start.14 = (bf16[1664,128]{1,0:T(8,128)(2,1)S(1)}, bf16[1664,128]{1,0:T(8,128)(2,1)S(1)}, u32[]{:S(2)}, u32[]{:S(2)}) collective-permute-start(bf16[1664,128]{1,0:T(8,128)(2,1)S(1)} %get-tuple-element.25), channel_id=1, source_target_pairs={{0,2},{2,4},{4,6},{6,8},{8,10},{10,12},{12,14},{14,16},{16,18},{18... | collective-permute-start | bytes 1277960 | tf_op jit(solution)/shard_map/ppermute | solution.py:229
  151.1 74.8 %collective-permute-start.16 = (bf16[1664,128]{1,0:T(8,128)(2,1)S(1)}, bf16[1664,128]{1,0:T(8,128)(2,1)S(1)}, u32[]{:S(2)}, u32[]{:S(2)}) collective-permute-start(bf16[1664,128]{1,0:T(8,128)(2,1)S(1)} %get-tuple-element.27), channel_id=1, source_target_pairs={{2,0},{4,2},{6,4},{8,6},{10,8},{12,10},{14,12},{16,14},{18,16},{20... | collective-permute-start | bytes 1277960 | tf_op jit(solution)/shard_map/ppermute | solution.py:229
  157.6 68.2 %collective-permute-start.15 = (bf16[1152,128]{1,0:T(8,128)(2,1)S(1)}, bf16[1152,128]{1,0:T(8,128)(2,1)S(1)}, u32[]{:S(2)}, u32[]{:S(2)}) collective-permute-start(bf16[1152,128]{1,0:T(8,128)(2,1)S(1)} %get-tuple-element.26), channel_id=1, source_target_pairs={{0,4},{2,6},{4,8},{6,10},{8,12},{10,14},{12,16},{14,18},{16,20},{1... | collective-permute-start | bytes 884744 | tf_op jit(solution)/shard_map/ppermute | solution.py:229
  159.6 66.3 %collective-permute-start.17 = (bf16[640,128]{1,0:T(8,128)(2,1)S(1)}, bf16[640,128]{1,0:T(8,128)(2,1)S(1)}, u32[]{:S(2)}, u32[]{:S(2)}) collective-permute-start(bf16[640,128]{1,0:T(8,128)(2,1)S(1)} %get-tuple-element.28), channel_id=1, source_target_pairs={{4,0},{6,2},{8,4},{10,6},{12,8},{14,10},{16,12},{18,14},{20,16},{2... | collective-permute-start | bytes 491528 | tf_op jit(solution)/shard_map/ppermute | solution.py:229
  167.7 5.5 %collective-permute-start.1 = (f32[8,128]{1,0:T(8,128)S(1)}, f32[8,128]{1,0:T(8,128)S(1)}, u32[]{:S(2)}, u32[]{:S(2)}) collective-permute-start(f32[8,128]{1,0:T(8,128)S(1)} %get-tuple-element.18), channel_id=1, source_target_pairs={{0,2},{2,0},{4,6},{6,4},{8,10},{10,8},{12,14},{14,12},{1,3},{3,1},... | collective-permute-start | bytes 12296 | tf_op jit(solution)/shard_map/ppermute | solution.py:237
  173.2 6.4 %collective-permute-start.2 = (f32[8,128]{1,0:T(8,128)S(1)}, f32[8,128]{1,0:T(8,128)S(1)}, u32[]{:S(2)}, u32[]{:S(2)}) collective-permute-start(f32[8,128]{1,0:T(8,128)S(1)} %add.35), channel_id=1, source_target_pairs={{0,4},{2,6},{4,0},{6,2},{8,12},{10,14},{12,8},{14,10},{1,5},{3,7},... | collective-permute-start | bytes 12296 | tf_op jit(solution)/shard_map/ppermute | solution.py:237
  179.6 9.4 %collective-permute-start.3 = (f32[8,128]{1,0:T(8,128)S(1)}, f32[8,128]{1,0:T(8,128)S(1)}, u32[]{:S(2)}, u32[]{:S(2)}) collective-permute-start(f32[8,128]{1,0:T(8,128)S(1)} %add.36), channel_id=1, source_target_pairs={{0,8},{2,10},{4,12},{6,14},{8,0},{10,2},{12,4},{14,6},{1,9},{3,11}... | collective-permute-start | bytes 12296 | tf_op jit(solution)/shard_map/ppermute | solution.py:237
  189.0 5.5 %collective-permute-start.4 = (f32[8,128]{1,0:T(8,128)S(1)}, f32[8,128]{1,0:T(8,128)S(1)}, u32[]{:S(2)}, u32[]{:S(2)}) collective-permute-start(f32[8,128]{1,0:T(8,128)S(1)} %add.37), channel_id=1, source_target_pairs={{0,16},{16,0},{32,48},{48,32},{64,80},{80,64},{96,112},{112,96},{1... | collective-permute-start | bytes 12296 | tf_op jit(solution)/shard_map/ppermute | solution.py:237
  194.5 6.4 %collective-permute-start.5 = (f32[8,128]{1,0:T(8,128)S(1)}, f32[8,128]{1,0:T(8,128)S(1)}, u32[]{:S(2)}, u32[]{:S(2)}) collective-permute-start(f32[8,128]{1,0:T(8,128)S(1)} %add.38), channel_id=1, source_target_pairs={{0,32},{16,48},{32,0},{48,16},{64,96},{80,112},{96,64},{112,80},{1... | collective-permute-start | bytes 12296 | tf_op jit(solution)/shard_map/ppermute | solution.py:237
  200.9 9.4 %collective-permute-start.6 = (f32[8,128]{1,0:T(8,128)S(1)}, f32[8,128]{1,0:T(8,128)S(1)}, u32[]{:S(2)}, u32[]{:S(2)}) collective-permute-start(f32[8,128]{1,0:T(8,128)S(1)} %add.39), channel_id=1, source_target_pairs={{0,64},{16,80},{32,96},{48,112},{64,0},{80,16},{96,32},{112,48},{1... | collective-permute-start | bytes 12296 | tf_op jit(solution)/shard_map/ppermute | solution.py:237
  210.3 3.0 %collective-permute-start.7 = (f32[8,128]{1,0:T(8,128)S(1)}, f32[8,128]{1,0:T(8,128)S(1)}, u32[]{:S(2)}, u32[]{:S(2)}) collective-permute-start(f32[8,128]{1,0:T(8,128)S(1)} %add.40), channel_id=1, source_target_pairs={{0,128},{128,0},{256,384},{384,256},{512,640},{640,512},{768,896},... | collective-permute-start | bytes 12296 | tf_op jit(solution)/shard_map/ppermute | solution.py:237
  213.4 5.5 %collective-permute-start.8 = (f32[8,128]{1,0:T(8,128)S(1)}, f32[8,128]{1,0:T(8,128)S(1)}, u32[]{:S(2)}, u32[]{:S(2)}) collective-permute-start(f32[8,128]{1,0:T(8,128)S(1)} %add.41), channel_id=1, source_target_pairs={{0,256},{128,384},{256,0},{384,128},{512,768},{640,896},{768,512},... | collective-permute-start | bytes 12296 | tf_op jit(solution)/shard_map/ppermute | solution.py:237
  218.9 7.0 %collective-permute-start.9 = (f32[8,128]{1,0:T(8,128)S(1)}, f32[8,128]{1,0:T(8,128)S(1)}, u32[]{:S(2)}, u32[]{:S(2)}) collective-permute-start(f32[8,128]{1,0:T(8,128)S(1)} %add.42), channel_id=1, source_target_pairs={{0,512},{128,640},{256,768},{384,896},{512,0},{640,128},{768,256},... | collective-permute-start | bytes 12296 | tf_op jit(solution)/shard_map/ppermute | solution.py:237
  229.0 29.6 %copy-start.1 = (bf16[16,256,128]{2,1,0:T(8,128)(2,1)S(1)}, bf16[16,256,128]{2,1,0:T(8,128)(2,1)}, u32[]{:S(2)}) copy-start(bf16[16,256,128]{2,1,0:T(8,128)(2,1)} %prow.3) | copy-start | bytes 3145732
  229.0 29.6 %copy-start.3 = (bf16[16,256,128]{2,1,0:T(8,128)(2,1)S(1)}, bf16[16,256,128]{2,1,0:T(8,128)(2,1)}, u32[]{:S(2)}) copy-start(bf16[16,256,128]{2,1,0:T(8,128)(2,1)} %pcol.3) | copy-start | bytes 3145732

commit v2 on v1

v2 whole, which is shorter than its diff:
```python
import functools

import jax
import jax.numpy as jnp
from jax import lax
from jax.experimental import pallas as pl
from jax.experimental.pallas import tpu as pltpu
from jax.sharding import Mesh, PartitionSpec as P

BW = 128
SLOTS = 8
HALF = 4
META = 16
CARRIED = 32
WIDE = 9 * BW
LINE = ("layer", "row", "ring")
F32 = jnp.float32
BF16 = jnp.bfloat16
VMEM = pl.BlockSpec(memory_space=pltpu.VMEM)
SMEM = pl.BlockSpec(memory_space=pltpu.SMEM)

REACH = {
    -1: [(-2, s) for s in range(2, 8)] + [(-1, s) for s in range(1, 8)],
    -2: [(-4, s) for s in range(4, 8)] + [(-3, s) for s in range(3, 8)],
    1: [(2, s) for s in range(0, 7)] + [(3, s) for s in range(0, 6)],
    2: [(4, s) for s in range(0, 5)],
}
SIDES = (-1, -2, 1, 2)
OWN = [(r, s) for r in range(2) for s in range(SLOTS)]


def call(kernel, out_shape, in_specs, out_specs, scratch=(), flops=0, moved=0):
    return pl.pallas_call(
        kernel,
        out_shape=out_shape,
        in_specs=in_specs,
        out_specs=out_specs,
        scratch_shapes=list(scratch),
        compiler_params=pltpu.CompilerParams(vmem_limit_bytes=24 * 1024 * 1024),
        cost_estimate=pl.CostEstimate(flops=flops, bytes_accessed=moved, transcendentals=0),
    )


def rows(block):
    return slice(block * BW, (block + 1) * BW)


def integrate(place, route, slot, w, prow, pcol, out_other, out_own, pos_out, made, count):
    batches, points, _ = prow.shape
    dests = out_own.shape[0]
    for t in range(2 * dests):
        count[t] = 0
    w_cols = jnp.concatenate([w[...], jnp.zeros((BW - batches, points), F32)], axis=0).T
    line = lax.broadcasted_iota(jnp.int32, (dests * META, BW), 0)
    named = jnp.where(line % META < 4, line // META * 4 + line % META, -1)
    labels = jnp.zeros((dests * META, BW), F32)
    for b in range(batches):
        t = route[b]
        rank = count[t]
        count[t] = rank + 1
        pos = t * 2 + jnp.minimum(rank, 1)
        pos_out[b] = pos
        labels = jnp.where(named == pos, (slot[b] + 1).astype(F32), labels)
    labels = labels.astype(BF16)
    for d in range(dests):
        out_own[d, 2 * BW :, :] = labels[d * META : (d + 1) * META]
        out_other[d, 2 * BW :, :] = labels[d * META : (d + 1) * META]
    for b in range(batches):
        scaled = (w_cols[:, b : b + 1] * pcol[b].astype(F32)).astype(BF16)
        value = lax.dot_general(
            prow[b], scaled, (((0,), (0,)), ((), ())), preferred_element_type=F32
        )
        made[b] = (value / points).astype(BF16)
    for b in range(batches):
        pos = pos_out[b]
        mine = pos // 2 % 2 == place[0]
        at = pl.multiple_of(pos % 2 * BW, BW)

        @pl.when(mine)
        def _():
            out_own[pos // 4, pl.ds(at, BW), :] = made[b]

        @pl.when(jnp.logical_not(mine))
        def _():
            out_other[pos // 4, pl.ds(at, BW), :] = made[b]


def accumulate(labels, arrived, out, total):
    total[...] = jnp.zeros_like(total)
    for i in range(2 * arrived.shape[0]):
        label = labels[i]

        @pl.when(label > 0)
        def _():
            total[label - 1] += arrived[i // 2, rows(i % 2), :].astype(F32)

    for s in range(SLOTS):
        out[rows(s), :] = total[s].astype(out.dtype)


def combine(place, ham_pattern, dens_pattern, own, other, ham, sums, *, pairs):
    column = 2 * place[1] + place[0] - HALF
    line = lax.broadcasted_iota(jnp.int32, (META, BW), 0)
    meta = jnp.zeros((META, BW), F32)
    square = jnp.zeros((BW, BW), F32)
    for s in range(SLOTS):
        meta = jnp.where(line == s, dens_pattern[0, s].astype(F32), meta)
        inside = (column + s >= 0) & (column + s < 2 * pairs)
        usable = jnp.where(inside, ham_pattern[0, s], 0).astype(F32)
        value = own[rows(s), :] + other[rows(s), :].astype(F32)
        block = (value * usable).astype(BF16)
        ham[rows(s), :] = block
        wide = block.astype(F32)
        square += wide * wide
        if s == HALF:
            diag = wide
    eye = lax.broadcasted_iota(jnp.int32, (BW, BW), 0) == lax.broadcasted_iota(
        jnp.int32, (BW, BW), 1
    )
    trace_sum = jnp.sum(jnp.where(eye, diag, 0.0), axis=(0, 1), keepdims=True)
    square_sum = jnp.sum(square, axis=(0, 1), keepdims=True)
    sums[...] = jnp.where(line[:SLOTS] == 0, trace_sum, square_sum)
    ham[SLOTS * BW :, :] = meta.astype(BF16)


def carried(sums):
    high = sums.astype(BF16).astype(F32)
    middle = (sums - high).astype(BF16).astype(F32)
    low = sums - high - middle
    return jnp.concatenate([high, middle, low, jnp.zeros_like(low)], axis=0).astype(BF16)


def brought(piece):
    parts = piece[piece.shape[0] - CARRIED :, :].astype(F32)
    return parts[:SLOTS] + parts[SLOTS : 2 * SLOTS] + parts[2 * SLOTS : 3 * SLOTS]


def spread(place, sums, own, other, ham, *outs):
    side, size = place[0], SLOTS * BW
    pieces, sums_out = outs[:4], outs[4]
    sums_out[...] = sums[...]
    ham[pl.ds(pl.multiple_of(side * size, size), size), :] = own[:size, :]
    ham[pl.ds(pl.multiple_of((1 - side) * size, size), size), :] = other[:size, :]
    mine, others = own[size:, :].astype(F32), other[size : size + META, :].astype(F32)
    masks = [jnp.where(side == r, mine, others)[:SLOTS] for r in range(2)]
    meta = jnp.concatenate(masks, axis=0).astype(BF16)
    ham[2 * size :, :] = meta
    deal(place, ham, pieces, meta)


def send_piece(source, piece, towards):
    for i, (b, s) in enumerate(REACH[-towards]):
        r = b + 2 * towards
        piece[rows(i), :] = source[rows(r * SLOTS + s), :]


def by_turn(place, step, act):
    behind = place[1] // step % 2
    pl.when(behind == 0)(lambda: act(step, -step))
    pl.when(behind != 0)(lambda: act(-step, step))


def deal(place, source, pieces, tail):
    for step, early, late in ((1, *pieces[:2]), (2, *pieces[2:])):

        def act(first, second, early=early, late=late):
            send_piece(source, early, first)
            send_piece(source, late, second)

        by_turn(place, step, act)
    for piece in pieces:
        piece[piece.shape[0] - tail.shape[0] :, :] = tail


def fill(place, right, ours, near, make):
    given = {(b, b + s - HALF) for b, s in OWN + sum(REACH.values(), [])}
    for b in range(-HALF, HALF + 1):
        for c in range(-HALF, HALF + 1):
            if (b, c) not in given:
                right[rows(b + HALF), rows(c + HALF)] = jnp.zeros((BW, BW), BF16)

    def lay(piece, blocks):
        for i, (b, s) in enumerate(blocks):
            right[rows(b + HALF), rows(b + s)] = make(piece, i, b, s)

    lay(ours, OWN)

    for step, early, late in ((1, *near[:2]), (2, *near[2:])):

        def act(first, second, early=early, late=late):
            lay(early, REACH[first])
            lay(late, REACH[second])

        by_turn(place, step, act)


def square_pair(right):
    left = right[HALF * BW : (HALF + 2) * BW, :]
    for j in range(3):
        span = slice(j * 3 * BW, (j + 1) * 3 * BW)
        yield j, jnp.dot(left, right[:, span], preferred_element_type=F32)


def first_square(place, sums, ham, *refs):
    near, out, pieces, right = refs[:4], refs[4], refs[5:9], refs[9]
    fill(place, right, ham, near, lambda piece, i, b, s: piece[rows(i), :])
    for j, made in square_pair(right):
        for i in range(3):
            for r in range(2):
                s = 3 * j + i - r
                if 0 <= s < SLOTS:
                    out[rows(r * SLOTS + s), :] = made[rows(r), rows(i)].astype(BF16)
    deal(place, out, pieces, carried(sums[...]))


def second_square(place, labels_own, labels_other, sums, ham, *refs, order):
    near, sq, near_sq = refs[:4], refs[4], refs[5:9]
    density, answers, right, blocks = refs[9:]
    side = place[0]
    total = sums[...] + brought(near_sq[0]) + brought(near_sq[1]) + brought(near_sq[2])
    average = total[0:1, :] / order
    spread = jnp.sqrt(total[1:2, :] / order - average * average + 1e-06)
    lift = 0.5 + average / (4.0 * spread)
    scaling = 1.0 / (4.0 * spread)
    unit, linear, quadratic = lift * lift, 2.0 * lift * scaling, scaling * scaling
    eye = lax.broadcasted_iota(jnp.int32, (BW, BW), 0) == lax.broadcasted_iota(
        jnp.int32, (BW, BW), 1
    )
    unit_block = jnp.where(eye, jnp.broadcast_to(unit, (BW, BW)), 0.0)
    squares = {id(ham): sq} | {id(h): g for h, g in zip(near, near_sq)}
    masks = {}
    for piece in (ham, *near):
        masks[id(piece)] = piece[piece.shape[0] - META :, :].astype(F32)

    def make(piece, i, b, s):
        line = b % 2 * SLOTS + s
        value = quadratic * squares[id(piece)][rows(i), :].astype(F32)
        value = value - linear * piece[rows(i), :].astype(F32)
        if s == HALF:
            value = value + unit_block
        return (value * masks[id(piece)][line : line + 1, :]).astype(BF16)

    fill(place, right, ham, near, make)
    mask = masks[id(ham)]
    for j, made in square_pair(right):
        for i in range(3):
            for r in range(2):
                s = 3 * j + i - r
                if 0 <= s < SLOTS:
                    k = r * SLOTS + s
                    first = right[rows(HALF + r), rows(3 * j + i)].astype(F32)
                    value = (2.0 * first - made[rows(r), rows(i)]) * mask[k : k + 1, :]
                    blocks[k] = value.astype(BF16)
    for s in range(SLOTS):
        density[:, rows(s)] = blocks[side * SLOTS + s]
    for labels, row in ((labels_own, side), (labels_other, 1 - side)):
        for i in range(2 * answers.shape[0]):
            label = jnp.maximum(labels[i], 1)
            at = pl.multiple_of((row * 2 + i % 2) * BW, BW)
            answers[i // 2, pl.ds(at, BW), :] = blocks[row * SLOTS + label - 1]


def on_grid(pos, returned, prow, pcol, out):
    batches, points, _ = prow.shape
    lane = lax.broadcasted_iota(jnp.int32, (points, BW), 1)
    values = jnp.zeros((points, BW), F32)
    for b in range(batches):
        at = pl.multiple_of(pos[b] % 4 * BW, BW)
        block = returned[pos[b] // 4, pl.ds(at, BW), :]
        partial = jnp.dot(prow[b], block, preferred_element_type=F32) * pcol[b].astype(F32)
        values = jnp.where(lane == b, jnp.sum(partial, axis=1, keepdims=True), values)
    out[...] = values.T[:batches, :]


def exchanged(pieces):
    count = lax.axis_size(LINE)
    got = []
    for piece, step, turn in zip(pieces, (1, 1, 2, 2), (0, 1, 0, 1)):
        hops = [(i, (i + step) % count) for i in range(count) if i // step % 2 == turn]
        got.append(lax.ppermute(piece, LINE, hops + [(b, a) for a, b in hops]))
    return got


def added_over(sums, *rounds):
    for axis, step in rounds:
        size = lax.axis_size(axis)
        if step < size:
            sums = sums + lax.ppermute(sums, axis, [(i, i ^ step) for i in range(size)])
    return sums


ROUNDS = (
    (("layer", 1), ("layer", 2), ("layer", 4), ("ring", 4), ("row", 1), ("row", 2), ("row", 4)),
    (("side", 1),),
)


def shards(phi_row, phi_col, weights, batch_route, batch_slot, ham_pattern, dens_pattern):
    batches, points, _ = phi_row.shape
    dests = lax.axis_size("ring")
    pairs = lax.axis_size(LINE)
    side = lax.axis_index("side")
    place = jnp.stack([side, lax.axis_index(LINE)]).astype(jnp.int32)
    depth = 2 * BW + META

    def shape(*dims, kind=BF16):
        return jax.ShapeDtypeStruct(dims, kind)

    out_other, out_own, position = call(
        integrate,
        (shape(dests, depth, BW), shape(dests, depth, BW), shape(batches, kind=jnp.int32)),
        [SMEM, SMEM, SMEM, VMEM, VMEM, VMEM],
        (VMEM, VMEM, SMEM),
        [
            pltpu.VMEM((batches, BW, BW), BF16),
            pltpu.SMEM((2 * dests,), jnp.int32),
        ],
        flops=2 * batches * points * BW * BW,
        moved=6 << 20,
    )(place, batch_route.reshape(batches), batch_slot, weights, phi_row, phi_col)

    def received(outgoing, parity, kind):
        arrived = lax.all_to_all(outgoing, "ring", split_axis=0, concat_axis=0, tiled=True)
        labels = arrived[:, 2 * BW : 2 * BW + 4, 0].astype(jnp.int32)
        labels = jnp.where(parity == 0, labels[:, :2], labels[:, 2:]).reshape(2 * dests)
        part = call(
            accumulate,
            shape(SLOTS * BW, BW, kind=kind),
            [SMEM, VMEM],
            VMEM,
            [pltpu.VMEM((SLOTS, BW, BW), F32)],
            moved=2 << 20,
        )(labels, arrived)
        return labels, part

    swap = [(0, 1), (1, 0)]
    labels_other, for_other = received(out_other, 1 - side, BF16)
    from_other = lax.ppermute(for_other, "side", swap)
    labels_own, part = received(out_own, side, F32)

    row_shape = shape(SLOTS * BW + META, BW)
    sums_shape = shape(SLOTS, BW, kind=F32)
    ham_own, sums = call(
        functools.partial(combine, pairs=pairs),
        (row_shape, sums_shape),
        [SMEM, SMEM, SMEM, VMEM, VMEM],
        (VMEM, VMEM),
        moved=2 << 20,
    )(place, ham_pattern, dens_pattern, part, from_other)
    ham_other = lax.ppermute(ham_own, "side", swap)
    sums = added_over(sums, *ROUNDS[0])
    sizes = [len(REACH[t]) * BW for t in (-1, -1, -2, -2)]
    ham, *pieces, sums = call(
        spread,
        (shape(2 * SLOTS * BW + META, BW),)
        + tuple(shape(n + META, BW) for n in sizes)
        + (sums_shape,),
        [SMEM, VMEM, VMEM, VMEM],
        (VMEM,) * 6,
        moved=4 << 20,
    )(place, sums, ham_own, ham_other)
    near = exchanged(pieces)
    sums = added_over(sums, *ROUNDS[1])

    sq, *pieces = call(
        first_square,
        (shape(2 * SLOTS * BW, BW),) + tuple(shape(n + CARRIED, BW) for n in sizes),
        [SMEM] + [VMEM] * 6,
        (VMEM,) * 5,
        [pltpu.VMEM((WIDE, WIDE), BF16)],
        flops=4 * BW * WIDE * WIDE,
        moved=4 << 20,
    )(place, sums, ham, *near)
    near_sq = exchanged(pieces)

    density, answers = call(
        functools.partial(second_square, order=2 * pairs * BW),
        (shape(BW, SLOTS * BW), shape(dests, 4 * BW, BW)),
        [SMEM] * 3 + [VMEM] * 11,
        (VMEM, VMEM),
        [pltpu.VMEM((WIDE, WIDE), BF16), pltpu.VMEM((2 * SLOTS, BW, BW), BF16)],
        flops=4 * BW * WIDE * WIDE,
        moved=6 << 20,
    )(place, labels_own, labels_other, sums, ham, *near, sq, *near_sq)
    returned = lax.all_to_all(answers, "ring", split_axis=0, concat_axis=0, tiled=True)

    grid_density = call(
        on_grid,
        shape(batches, points, kind=F32),
        [SMEM, VMEM, VMEM, VMEM],
        VMEM,
        flops=2 * batches * points * BW * BW,
        moved=6 << 20,
    )(position, returned, phi_row, phi_col)
    return (density, grid_density)


def solution(mesh):
    layer, row, col = (mesh.shape[a] for a in ("layer", "row", "col"))
    split = Mesh(
        mesh.devices.reshape(layer, row, col // 2, 2), ("layer", "row", "ring", "side")
    )
    axes = ("layer", "row", "ring", "side")
    in_specs = (
        P(axes, None, None),
        P(axes, None, None),
        P(axes, None),
        P(axes, None),
        P(axes),
        P(axes, None),
        P(axes, None),
    )
    out_specs = (P(axes, None), P(axes, None))
    return jax.shard_map(
        shards, mesh=split, in_specs=in_specs, out_specs=out_specs, check_vma=False
    )
```

time: 261 us -> 252 us (0.966)
  the two profiles are of different devices: /device:TPU:770 before, /device:TPU:6 now
where the time goes in v2:
time: 252 us; the launch traced here: 250 us
  starting transfers between devices  100 us (40%)
  waiting for transfers between devices  76 us (30%)
  blocking collectives  55.4 us (22%)
  Pallas kernels  13.8 us (5%)
  local copies, waits for them, and re-layouts  3.67 us (1%)
    ppermute x8, starting transfers between devices, exchanged(): got.append(lax.ppermute(piece, LINE, hops + [(b, a) for a, b in hops]))  33.3 us
    ppermute x8, waiting for transfers between devices, added_over(): sums = sums + lax.ppermute(sums, axis, [(i, i ^ step) for i in range(size)])  31.8 us
    ppermute x8, starting transfers between devices, added_over(): sums = sums + lax.ppermute(sums, axis, [(i, i ^ step) for i in range(size)])  30.9 us
    all_to_all x1, blocking collectives, shards(): lax.all_to_all(answers, 'ring', split_axis=0, concat_axis=0, tiled=True)  30.3 us
    ppermute x8, waiting for transfers between devices, exchanged(): got.append(lax.ppermute(piece, LINE, hops + [(b, a) for a, b in hops]))  26 us
    all_to_all x1, blocking collectives, received(): lax.all_to_all(outgoing, 'ring', split_axis=0, concat_axis=0, tiled=True)  25.1 us
    ppermute x1, starting transfers between devices, shards(): from_other = lax.ppermute(for_other, 'side', swap)  19.4 us
    ppermute x1, waiting for transfers between devices, shards(): from_other = lax.ppermute(for_other, 'side', swap)  18.2 us
  transfers between devices with their start and end apart: 19, of which 12 were waited for; matrix products, arithmetic and copies ran while one was open for 0% of the time, Pallas kernels for 1%

profile of v2, /device:TPU:6, one launch (start us, length us, event | category | flops | bytes accessed | tf_op | source)
XLA Modules:
  0.0 250.1 jit_solution(12587323275607616731)
XLA Ops:
  0.7 0.6 copy-done.4
  1.4 1.2 copy-done
  2.6 1.2 copy-done.2
  3.8 2.9 %shard_map.86 = (bf16[8,272,128]{2,1,0:T(8,128)(2,1)S(1)}, bf16[8,272,128]{2,1,0:T(8,128)(2,1)}, s32[16]{0:T(128)S(1)}) custom-call(s32[2]{0:T(128)S(1)} %pad_add_fusion.place, s32[16]{0:T(128)S(1)} %bitcast.5, s32[16]{0:T(128)S(1)} %copy-done.6, f32[16,256]{1,0:T(8,128)S(1)} %copy-done.4, bf16[16,256,128]{2,1,0:T(8,128)(2,1)S(1)} %copy-done, ...), custom_call_target="tpu_custom_call" | custom-call | flops 134217728 | bytes 6291456 | tf_op jit(solution)/shard_map/pallas_call | solution.py:309
  6.8 25.1 %all_to_all.15.arrived = bf16[8,272,128]{2,1,0:T(8,128)(2,1)S(1)} all-to-all(bf16[8,272,128]{2,1,0:T(8,128)(2,1)S(1)} %get-tuple-element.21), channel_id=1, replica_groups=mesh['layer'=8,'row'=8,'ring'=8,'side'=2] {'ring'}, dimensions={0} | all-to-all | bytes 1114112 | tf_op jit(solution)/shard_map/all_to_all | solution.py:323
  31.9 3.5 %all-to-all-start = ((bf16[8,272,128]{2,1,0:T(8,128)(2,1)}), bf16[8,272,128]{2,1,0:T(8,128)(2,1)S(1)}, u32[]{:S(2)}, u32[]{:S(2)}) async-start(bf16[8,272,128]{2,1,0:T(8,128)(2,1)} %get-tuple-element.20), calls=%async_computation | async-start | bytes 1114112 | tf_op jit(solution)/shard_map/all_to_all | solution.py:323
  35.5 0.1 copy.19
  35.6 0.1 copy.20
  35.7 0.8 shard_map.88
  36.5 19.4 %collective-permute-start = (bf16[1024,128]{1,0:T(8,128)(2,1)S(1)}, bf16[1024,128]{1,0:T(8,128)(2,1)S(1)}, u32[]{:S(2)}, u32[]{:S(2)}) collective-permute-start(bf16[1024,128]{1,0:T(8,128)(2,1)S(1)} %shard_map.88), channel_id=1, source_target_pairs={{0,1},{1,0},{2,3},{3,2},{4,5},{5,4},{6,7},{7,6},{8,9},{9,8},{10,11... | collective-permute-start | bytes 786440 | tf_op jit(solution)/shard_map/ppermute | solution.py:338
  55.9 0.1 copy.17
  56.0 0.1 copy.18
  56.2 0.8 shard_map.87.own
  56.9 18.2 %collective-permute-done.other = bf16[1024,128]{1,0:T(8,128)(2,1)S(1)} collective-permute-done((bf16[1024,128]{1,0:T(8,128)(2,1)S(1)}, bf16[1024,128]{1,0:T(8,128)(2,1)S(1)}, u32[]{:S(2)}, u32[]{:S(2)}) %collective-permute-start) | collective-permute-done | bytes 262176 | tf_op jit(solution)/shard_map/ppermute | solution.py:338
  75.2 0.8 shard_map.89
  76.0 13.3 %collective-permute-start.8 = (bf16[1040,128]{1,0:T(8,128)(2,1)S(1)}, bf16[1040,128]{1,0:T(8,128)(2,1)S(1)}, u32[]{:S(2)}, u32[]{:S(2)}) collective-permute-start(bf16[1040,128]{1,0:T(8,128)(2,1)S(1)} %get-tuple-element.23.own), channel_id=1, source_target_pairs={{0,1},{1,0},{2,3},{3,2},{4,5},{5,4},{6,7},{7,6},{8,9},{9,8},{10,11... | collective-permute-start | bytes 798728 | tf_op jit(solution)/shard_map/ppermute | solution.py:350
  89.3 1.9 collective-permute-start.1
  91.2 1.1 collective-permute-done.1
  92.3 2.7 %collective-permute-start.2 = (f32[8,128]{1,0:T(8,128)S(1)}, f32[8,128]{1,0:T(8,128)S(1)}, u32[]{:S(2)}, u32[]{:S(2)}) collective-permute-start(f32[8,128]{1,0:T(8,128)S(1)} %add.32), channel_id=1, source_target_pairs={{0,256},{128,384},{256,0},{384,128},{512,768},{640,896},{768,512},... | collective-permute-start | bytes 12296 | tf_op jit(solution)/shard_map/ppermute | solution.py:288
  95.1 2.7 %collective-permute-done.2 = f32[8,128]{1,0:T(8,128)S(1)} collective-permute-done((f32[8,128]{1,0:T(8,128)S(1)}, f32[8,128]{1,0:T(8,128)S(1)}, u32[]{:S(2)}, u32[]{:S(2)}) %collective-permute-start.2) | collective-permute-done | bytes 4128 | tf_op jit(solution)/shard_map/ppermute | solution.py:288
  97.8 3.3 %collective-permute-start.3 = (f32[8,128]{1,0:T(8,128)S(1)}, f32[8,128]{1,0:T(8,128)S(1)}, u32[]{:S(2)}, u32[]{:S(2)}) collective-permute-start(f32[8,128]{1,0:T(8,128)S(1)} %add.33), channel_id=1, source_target_pairs={{0,512},{128,640},{256,768},{384,896},{512,0},{640,128},{768,256},... | collective-permute-start | bytes 12296 | tf_op jit(solution)/shard_map/ppermute | solution.py:288
  101.1 3.7 %collective-permute-done.3 = f32[8,128]{1,0:T(8,128)S(1)} collective-permute-done((f32[8,128]{1,0:T(8,128)S(1)}, f32[8,128]{1,0:T(8,128)S(1)}, u32[]{:S(2)}, u32[]{:S(2)}) %collective-permute-start.3) | collective-permute-done | bytes 4128 | tf_op jit(solution)/shard_map/ppermute | solution.py:288
  104.8 7.5 %collective-permute-start.4 = (f32[8,128]{1,0:T(8,128)S(1)}, f32[8,128]{1,0:T(8,128)S(1)}, u32[]{:S(2)}, u32[]{:S(2)}) collective-permute-start(f32[8,128]{1,0:T(8,128)S(1)} %add.34), channel_id=1, source_target_pairs={{0,8},{2,10},{4,12},{6,14},{8,0},{10,2},{12,4},{14,6},{1,9},{3,11}... | collective-permute-start | bytes 12296 | tf_op jit(solution)/shard_map/ppermute | solution.py:288
  112.4 1.9 collective-permute-done.4
  114.2 4.4 %collective-permute-start.5 = (f32[8,128]{1,0:T(8,128)S(1)}, f32[8,128]{1,0:T(8,128)S(1)}, u32[]{:S(2)}, u32[]{:S(2)}) collective-permute-start(f32[8,128]{1,0:T(8,128)S(1)} %add.35), channel_id=1, source_target_pairs={{0,16},{16,0},{32,48},{48,32},{64,80},{80,64},{96,112},{112,96},{1... | collective-permute-start | bytes 12296 | tf_op jit(solution)/shard_map/ppermute | solution.py:288
  118.6 1.6 collective-permute-done.5
  120.1 2.6 %collective-permute-start.6 = (f32[8,128]{1,0:T(8,128)S(1)}, f32[8,128]{1,0:T(8,128)S(1)}, u32[]{:S(2)}, u32[]{:S(2)}) collective-permute-start(f32[8,128]{1,0:T(8,128)S(1)} %add.36), channel_id=1, source_target_pairs={{0,32},{16,48},{32,0},{48,16},{64,96},{80,112},{96,64},{112,80},{1... | collective-permute-start | bytes 12296 | tf_op jit(solution)/shard_map/ppermute | solution.py:288
  122.7 3.8 %collective-permute-done.6 = f32[8,128]{1,0:T(8,128)S(1)} collective-permute-done((f32[8,128]{1,0:T(8,128)S(1)}, f32[8,128]{1,0:T(8,128)S(1)}, u32[]{:S(2)}, u32[]{:S(2)}) %collective-permute-start.6) | collective-permute-done | bytes 4128 | tf_op jit(solution)/shard_map/ppermute | solution.py:288
  126.5 6.1 %collective-permute-start.7 = (f32[8,128]{1,0:T(8,128)S(1)}, f32[8,128]{1,0:T(8,128)S(1)}, u32[]{:S(2)}, u32[]{:S(2)}) collective-permute-start(f32[8,128]{1,0:T(8,128)S(1)} %add.37), channel_id=1, source_target_pairs={{0,64},{16,80},{32,96},{48,112},{64,0},{80,16},{96,32},{112,48},{1... | collective-permute-start | bytes 12296 | tf_op jit(solution)/shard_map/ppermute | solution.py:288
  132.6 3.3 %collective-permute-done.7 = f32[8,128]{1,0:T(8,128)S(1)} collective-permute-done((f32[8,128]{1,0:T(8,128)S(1)}, f32[8,128]{1,0:T(8,128)S(1)}, u32[]{:S(2)}, u32[]{:S(2)}) %collective-permute-start.7) | collective-permute-done | bytes 4128 | tf_op jit(solution)/shard_map/ppermute | solution.py:288
  135.9 0.7 shard_map.90
  136.7 3.7 %collective-permute-start.10 = (bf16[1680,128]{1,0:T(8,128)(2,1)S(1)}, bf16[1680,128]{1,0:T(8,128)(2,1)S(1)}, u32[]{:S(2)}, u32[]{:S(2)}) collective-permute-start(bf16[1680,128]{1,0:T(8,128)(2,1)S(1)} %get-tuple-element.26), channel_id=1, source_target_pairs={{0,2},{4,6},{8,10},{12,14},{16,18},{20,22},{24,26},{28,30},{32,34}... | collective-permute-start | bytes 1290248 | tf_op jit(solution)/shard_map/ppermute | solution.py:280
  140.4 3.3 %collective-permute-start.11 = (bf16[1680,128]{1,0:T(8,128)(2,1)S(1)}, bf16[1680,128]{1,0:T(8,128)(2,1)S(1)}, u32[]{:S(2)}, u32[]{:S(2)}) collective-permute-start(bf16[1680,128]{1,0:T(8,128)(2,1)S(1)} %get-tuple-element.27), channel_id=1, source_target_pairs={{2,4},{6,8},{10,12},{14,16},{18,20},{22,24},{26,28},{30,32},{34,36... | collective-permute-start | bytes 1290248 | tf_op jit(solution)/shard_map/ppermute | solution.py:280
  143.7 2.8 %collective-permute-start.12 = (bf16[1168,128]{1,0:T(8,128)(2,1)S(1)}, bf16[1168,128]{1,0:T(8,128)(2,1)S(1)}, u32[]{:S(2)}, u32[]{:S(2)}) collective-permute-start(bf16[1168,128]{1,0:T(8,128)(2,1)S(1)} %get-tuple-element.28), channel_id=1, source_target_pairs={{0,4},{2,6},{8,12},{10,14},{16,20},{18,22},{24,28},{26,30},{32,36}... | collective-permute-start | bytes 897032 | tf_op jit(solution)/shard_map/ppermute | solution.py:280
  146.6 3.3 %collective-permute-start.13 = (bf16[1168,128]{1,0:T(8,128)(2,1)S(1)}, bf16[1168,128]{1,0:T(8,128)(2,1)S(1)}, u32[]{:S(2)}, u32[]{:S(2)}) collective-permute-start(bf16[1168,128]{1,0:T(8,128)(2,1)S(1)} %get-tuple-element.29), channel_id=1, source_target_pairs={{4,8},{6,10},{12,16},{14,18},{20,24},{22,26},{28,32},{30,34},{36,4... | collective-permute-start | bytes 897032 | tf_op jit(solution)/shard_map/ppermute | solution.py:280
  149.9 2.4 collective-permute-start.9
  152.3 13.6 %collective-permute-done.9 = f32[8,128]{1,0:T(8,128)S(1)} collective-permute-done((f32[8,128]{1,0:T(8,128)S(1)}, f32[8,128]{1,0:T(8,128)S(1)}, u32[]{:S(2)}, u32[]{:S(2)}) %collective-permute-start.9) | collective-permute-done | bytes 4128 | tf_op jit(solution)/shard_map/ppermute | solution.py:288
  165.9 2.7 %collective-permute-done.13.refs_3_ = bf16[1168,128]{1,0:T(8,128)(2,1)S(1)} collective-permute-done((bf16[1168,128]{1,0:T(8,128)(2,1)S(1)}, bf16[1168,128]{1,0:T(8,128)(2,1)S(1)}, u32[]{:S(2)}, u32[]{:S(2)}) %collective-permute-start.13) | collective-permute-done | bytes 299040 | tf_op jit(solution)/shard_map/ppermute | solution.py:280
  168.6 2.2 shard_map.91
  170.9 7.1 %collective-permute-start.14 = (bf16[1696,128]{1,0:T(8,128)(2,1)S(1)}, bf16[1696,128]{1,0:T(8,128)(2,1)S(1)}, u32[]{:S(2)}, u32[]{:S(2)}) collective-permute-start(bf16[1696,128]{1,0:T(8,128)(2,1)S(1)} %get-tuple-element.31), channel_id=1, source_target_pairs={{0,2},{4,6},{8,10},{12,14},{16,18},{20,22},{24,26},{28,30},{32,34}... | collective-permute-start | bytes 1302536 | tf_op jit(solution)/shard_map/ppermute | solution.py:280
  178.0 8.0 %collective-permute-start.15 = (bf16[1696,128]{1,0:T(8,128)(2,1)S(1)}, bf16[1696,128]{1,0:T(8,128)(2,1)S(1)}, u32[]{:S(2)}, u32[]{:S(2)}) collective-permute-start(bf16[1696,128]{1,0:T(8,128)(2,1)S(1)} %get-tuple-element.32), channel_id=1, source_target_pairs={{2,4},{6,8},{10,12},{14,16},{18,20},{22,24},{26,28},{30,32},{34,36... | collective-permute-start | bytes 1302536 | tf_op jit(solution)/shard_map/ppermute | solution.py:280
  186.0 1.9 collective-permute-start.16
  187.9 3.1 %collective-permute-start.17 = (bf16[1184,128]{1,0:T(8,128)(2,1)S(1)}, bf16[1184,128]{1,0:T(8,128)(2,1)S(1)}, u32[]{:S(2)}, u32[]{:S(2)}) collective-permute-start(bf16[1184,128]{1,0:T(8,128)(2,1)S(1)} %get-tuple-element.34), channel_id=1, source_target_pairs={{4,8},{6,10},{12,16},{14,18},{20,24},{22,26},{28,32},{30,34},{36,4... | collective-permute-start | bytes 909320 | tf_op jit(solution)/shard_map/ppermute | solution.py:280
  191.0 13.4 %collective-permute-done.16.refs_7_ = bf16[1184,128]{1,0:T(8,128)(2,1)S(1)} collective-permute-done((bf16[1184,128]{1,0:T(8,128)(2,1)S(1)}, bf16[1184,128]{1,0:T(8,128)(2,1)S(1)}, u32[]{:S(2)}, u32[]{:S(2)}) %collective-permute-start.16) | collective-permute-done | bytes 303136 | tf_op jit(solution)/shard_map/ppermute | solution.py:280
  204.5 9.8 %collective-permute-done.17.refs_8_ = bf16[1184,128]{1,0:T(8,128)(2,1)S(1)} collective-permute-done((bf16[1184,128]{1,0:T(8,128)(2,1)S(1)}, bf16[1184,128]{1,0:T(8,128)(2,1)S(1)}, u32[]{:S(2)}, u32[]{:S(2)}) %collective-permute-start.17) | collective-permute-done | bytes 303136 | tf_op jit(solution)/shard_map/ppermute | solution.py:280
  214.3 3.5 %shard_map.92 = (bf16[128,1024]{1,0:T(8,128)(2,1)}, bf16[8,512,128]{2,1,0:T(8,128)(2,1)S(1)}) custom-call(s32[2]{0:T(128)S(1)} %pad_add_fusion.place, s32[16]{0:T(128)S(1)} %reshape.18.labels.labels_own, s32[16]{0:T(128)S(1)} %reshape.19.labels.labels_other, f32[8,128]{1,0:T(8,128)S(1)} %add.39.sums, bf16[2064,128]{1,0:T(8,128)(2,1)S(1)} %get-tuple-element.25.ham, ...), custom_call_target="tpu_custom_call" | custom-call | flops 679477248 | bytes 6291456 | tf_op jit(solution)/shard_map/pallas_call | solution.py:376
  217.8 30.3 %all_to_all.16.returned = bf16[8,512,128]{2,1,0:T(8,128)(2,1)S(1)} all-to-all(bf16[8,512,128]{2,1,0:T(8,128)(2,1)S(1)} %get-tuple-element.37), channel_id=1, replica_groups=mesh['layer'=8,'row'=8,'ring'=8,'side'=2] {'ring'}, dimensions={0} | all-to-all | bytes 2097152 | tf_op jit(solution)/shard_map/all_to_all | solution.py:385
  248.1 2.0 shard_map.93
  (37 shorter events, 0.4 us)
Async XLA Ops:
  0.6 0.7 copy-start.4
  0.7 0.7 copy-start.5
  0.7 0.7 copy-start.6
  1.4 1.2 copy-start
  2.6 1.2 copy-start.2
  31.9 24.0 %all-to-all-start = ((bf16[8,272,128]{2,1,0:T(8,128)(2,1)}), bf16[8,272,128]{2,1,0:T(8,128)(2,1)S(1)}, u32[]{:S(2)}, u32[]{:S(2)}) async-start(bf16[8,272,128]{2,1,0:T(8,128)(2,1)} %get-tuple-element.20), calls=%async_computation | async-start | bytes 1114112 | tf_op jit(solution)/shard_map/all_to_all | solution.py:323
  36.5 38.7 %collective-permute-start = (bf16[1024,128]{1,0:T(8,128)(2,1)S(1)}, bf16[1024,128]{1,0:T(8,128)(2,1)S(1)}, u32[]{:S(2)}, u32[]{:S(2)}) collective-permute-start(bf16[1024,128]{1,0:T(8,128)(2,1)S(1)} %shard_map.88), channel_id=1, source_target_pairs={{0,1},{1,0},{2,3},{3,2},{4,5},{5,4},{6,7},{7,6},{8,9},{9,8},{10,11... | collective-permute-start | bytes 786440 | tf_op jit(solution)/shard_map/ppermute | solution.py:338
  56.2 19.0 %copy-start.7 = (s32[1,8]{1,0:T(1,128)S(1)}, s32[1,8]{1,0:T(1,128)}, u32[]{:S(2)}) copy-start(s32[1,8]{1,0:T(1,128)} %ham_pattern.1) | copy-start | bytes 100
  56.2 19.0 %copy-start.8 = (s32[1,8]{1,0:T(1,128)S(1)}, s32[1,8]{1,0:T(1,128)}, u32[]{:S(2)}) copy-start(s32[1,8]{1,0:T(1,128)} %dens_pattern.1) | copy-start | bytes 100
  76.0 60.0 %collective-permute-start.8 = (bf16[1040,128]{1,0:T(8,128)(2,1)S(1)}, bf16[1040,128]{1,0:T(8,128)(2,1)S(1)}, u32[]{:S(2)}, u32[]{:S(2)}) collective-permute-start(bf16[1040,128]{1,0:T(8,128)(2,1)S(1)} %get-tuple-element.23.own), channel_id=1, source_target_pairs={{0,1},{1,0},{2,3},{3,2},{4,5},{5,4},{6,7},{7,6},{8,9},{9,8},{10,11... | collective-permute-start | bytes 798728 | tf_op jit(solution)/shard_map/ppermute | solution.py:350
  89.3 3.1 %collective-permute-start.1 = (f32[8,128]{1,0:T(8,128)S(1)}, f32[8,128]{1,0:T(8,128)S(1)}, u32[]{:S(2)}, u32[]{:S(2)}) collective-permute-start(f32[8,128]{1,0:T(8,128)S(1)} %get-tuple-element.22), channel_id=1, source_target_pairs={{0,128},{128,0},{256,384},{384,256},{512,640},{640,512},{768,896},... | collective-permute-start | bytes 12296 | tf_op jit(solution)/shard_map/ppermute | solution.py:288
  92.3 5.5 %collective-permute-start.2 = (f32[8,128]{1,0:T(8,128)S(1)}, f32[8,128]{1,0:T(8,128)S(1)}, u32[]{:S(2)}, u32[]{:S(2)}) collective-permute-start(f32[8,128]{1,0:T(8,128)S(1)} %add.32), channel_id=1, source_target_pairs={{0,256},{128,384},{256,0},{384,128},{512,768},{640,896},{768,512},... | collective-permute-start | bytes 12296 | tf_op jit(solution)/shard_map/ppermute | solution.py:288
  97.8 7.0 %collective-permute-start.3 = (f32[8,128]{1,0:T(8,128)S(1)}, f32[8,128]{1,0:T(8,128)S(1)}, u32[]{:S(2)}, u32[]{:S(2)}) collective-permute-start(f32[8,128]{1,0:T(8,128)S(1)} %add.33), channel_id=1, source_target_pairs={{0,512},{128,640},{256,768},{384,896},{512,0},{640,128},{768,256},... | collective-permute-start | bytes 12296 | tf_op jit(solution)/shard_map/ppermute | solution.py:288
  104.8 9.4 %collective-permute-start.4 = (f32[8,128]{1,0:T(8,128)S(1)}, f32[8,128]{1,0:T(8,128)S(1)}, u32[]{:S(2)}, u32[]{:S(2)}) collective-permute-start(f32[8,128]{1,0:T(8,128)S(1)} %add.34), channel_id=1, source_target_pairs={{0,8},{2,10},{4,12},{6,14},{8,0},{10,2},{12,4},{14,6},{1,9},{3,11}... | collective-permute-start | bytes 12296 | tf_op jit(solution)/shard_map/ppermute | solution.py:288
  114.2 5.9 %collective-permute-start.5 = (f32[8,128]{1,0:T(8,128)S(1)}, f32[8,128]{1,0:T(8,128)S(1)}, u32[]{:S(2)}, u32[]{:S(2)}) collective-permute-start(f32[8,128]{1,0:T(8,128)S(1)} %add.35), channel_id=1, source_target_pairs={{0,16},{16,0},{32,48},{48,32},{64,80},{80,64},{96,112},{112,96},{1... | collective-permute-start | bytes 12296 | tf_op jit(solution)/shard_map/ppermute | solution.py:288
  120.1 6.4 %collective-permute-start.6 = (f32[8,128]{1,0:T(8,128)S(1)}, f32[8,128]{1,0:T(8,128)S(1)}, u32[]{:S(2)}, u32[]{:S(2)}) collective-permute-start(f32[8,128]{1,0:T(8,128)S(1)} %add.36), channel_id=1, source_target_pairs={{0,32},{16,48},{32,0},{48,16},{64,96},{80,112},{96,64},{112,80},{1... | collective-permute-start | bytes 12296 | tf_op jit(solution)/shard_map/ppermute | solution.py:288
  126.5 9.4 %collective-permute-start.7 = (f32[8,128]{1,0:T(8,128)S(1)}, f32[8,128]{1,0:T(8,128)S(1)}, u32[]{:S(2)}, u32[]{:S(2)}) collective-permute-start(f32[8,128]{1,0:T(8,128)S(1)} %add.37), channel_id=1, source_target_pairs={{0,64},{16,80},{32,96},{48,112},{64,0},{80,16},{96,32},{112,48},{1... | collective-permute-start | bytes 12296 | tf_op jit(solution)/shard_map/ppermute | solution.py:288
  136.7 32.0 %collective-permute-start.10 = (bf16[1680,128]{1,0:T(8,128)(2,1)S(1)}, bf16[1680,128]{1,0:T(8,128)(2,1)S(1)}, u32[]{:S(2)}, u32[]{:S(2)}) collective-permute-start(bf16[1680,128]{1,0:T(8,128)(2,1)S(1)} %get-tuple-element.26), channel_id=1, source_target_pairs={{0,2},{4,6},{8,10},{12,14},{16,18},{20,22},{24,26},{28,30},{32,34}... | collective-permute-start | bytes 1290248 | tf_op jit(solution)/shard_map/ppermute | solution.py:280
  140.4 28.2 %collective-permute-start.11 = (bf16[1680,128]{1,0:T(8,128)(2,1)S(1)}, bf16[1680,128]{1,0:T(8,128)(2,1)S(1)}, u32[]{:S(2)}, u32[]{:S(2)}) collective-permute-start(bf16[1680,128]{1,0:T(8,128)(2,1)S(1)} %get-tuple-element.27), channel_id=1, source_target_pairs={{2,4},{6,8},{10,12},{14,16},{18,20},{22,24},{26,28},{30,32},{34,36... | collective-permute-start | bytes 1290248 | tf_op jit(solution)/shard_map/ppermute | solution.py:280
  143.7 22.2 %collective-permute-start.12 = (bf16[1168,128]{1,0:T(8,128)(2,1)S(1)}, bf16[1168,128]{1,0:T(8,128)(2,1)S(1)}, u32[]{:S(2)}, u32[]{:S(2)}) collective-permute-start(bf16[1168,128]{1,0:T(8,128)(2,1)S(1)} %get-tuple-element.28), channel_id=1, source_target_pairs={{0,4},{2,6},{8,12},{10,14},{16,20},{18,22},{24,28},{26,30},{32,36}... | collective-permute-start | bytes 897032 | tf_op jit(solution)/shard_map/ppermute | solution.py:280
  146.6 22.1 %collective-permute-start.13 = (bf16[1168,128]{1,0:T(8,128)(2,1)S(1)}, bf16[1168,128]{1,0:T(8,128)(2,1)S(1)}, u32[]{:S(2)}, u32[]{:S(2)}) collective-permute-start(bf16[1168,128]{1,0:T(8,128)(2,1)S(1)} %get-tuple-element.29), channel_id=1, source_target_pairs={{4,8},{6,10},{12,16},{14,18},{20,24},{22,26},{28,32},{30,34},{36,4... | collective-permute-start | bytes 897032 | tf_op jit(solution)/shard_map/ppermute | solution.py:280
  149.9 16.0 %collective-permute-start.9 = (f32[8,128]{1,0:T(8,128)S(1)}, f32[8,128]{1,0:T(8,128)S(1)}, u32[]{:S(2)}, u32[]{:S(2)}) collective-permute-start(f32[8,128]{1,0:T(8,128)S(1)} %get-tuple-element.24), channel_id=1, source_target_pairs={{0,1},{1,0},{2,3},{3,2},{4,5},{5,4},{6,7},{7,6},{8,9},{9,8},{10,11... | collective-permute-start | bytes 12296 | tf_op jit(solution)/shard_map/ppermute | solution.py:288
  170.9 43.4 %collective-permute-start.14 = (bf16[1696,128]{1,0:T(8,128)(2,1)S(1)}, bf16[1696,128]{1,0:T(8,128)(2,1)S(1)}, u32[]{:S(2)}, u32[]{:S(2)}) collective-permute-start(bf16[1696,128]{1,0:T(8,128)(2,1)S(1)} %get-tuple-element.31), channel_id=1, source_target_pairs={{0,2},{4,6},{8,10},{12,14},{16,18},{20,22},{24,26},{28,30},{32,34}... | collective-permute-start | bytes 1302536 | tf_op jit(solution)/shard_map/ppermute | solution.py:280
  178.0 36.3 %collective-permute-start.15 = (bf16[1696,128]{1,0:T(8,128)(2,1)S(1)}, bf16[1696,128]{1,0:T(8,128)(2,1)S(1)}, u32[]{:S(2)}, u32[]{:S(2)}) collective-permute-start(bf16[1696,128]{1,0:T(8,128)(2,1)S(1)} %get-tuple-element.32), channel_id=1, source_target_pairs={{2,4},{6,8},{10,12},{14,16},{18,20},{22,24},{26,28},{30,32},{34,36... | collective-permute-start | bytes 1302536 | tf_op jit(solution)/shard_map/ppermute | solution.py:280
  186.0 18.4 %collective-permute-start.16 = (bf16[1184,128]{1,0:T(8,128)(2,1)S(1)}, bf16[1184,128]{1,0:T(8,128)(2,1)S(1)}, u32[]{:S(2)}, u32[]{:S(2)}) collective-permute-start(bf16[1184,128]{1,0:T(8,128)(2,1)S(1)} %get-tuple-element.33), channel_id=1, source_target_pairs={{0,4},{2,6},{8,12},{10,14},{16,20},{18,22},{24,28},{26,30},{32,36}... | collective-permute-start | bytes 909320 | tf_op jit(solution)/shard_map/ppermute | solution.py:280
  187.9 26.3 %collective-permute-start.17 = (bf16[1184,128]{1,0:T(8,128)(2,1)S(1)}, bf16[1184,128]{1,0:T(8,128)(2,1)S(1)}, u32[]{:S(2)}, u32[]{:S(2)}) collective-permute-start(bf16[1184,128]{1,0:T(8,128)(2,1)S(1)} %get-tuple-element.34), channel_id=1, source_target_pairs={{4,8},{6,10},{12,16},{14,18},{20,24},{22,26},{28,32},{30,34},{36,4... | collective-permute-start | bytes 909320 | tf_op jit(solution)/shard_map/ppermute | solution.py:280
  217.8 30.3 %copy-start.1 = (bf16[16,256,128]{2,1,0:T(8,128)(2,1)S(1)}, bf16[16,256,128]{2,1,0:T(8,128)(2,1)}, u32[]{:S(2)}) copy-start(bf16[16,256,128]{2,1,0:T(8,128)(2,1)} %prow.3) | copy-start | bytes 3145732
  217.8 30.3 %copy-start.3 = (bf16[16,256,128]{2,1,0:T(8,128)(2,1)S(1)}, bf16[16,256,128]{2,1,0:T(8,128)(2,1)}, u32[]{:S(2)}) copy-start(bf16[16,256,128]{2,1,0:T(8,128)(2,1)} %pcol.3) | copy-start | bytes 3145732

commit v3 on v2

--- a/solution.py
+++ b/solution.py
@@ -135,10 +135,16 @@
     return parts[:SLOTS] + parts[SLOTS : 2 * SLOTS] + parts[2 * SLOTS : 3 * SLOTS]
 
 
+def hold(sums, source, out):
+    size = source.shape[0]
+    out[:size, :] = source[...]
+    out[size:, :] = carried(sums[...])
+
+
 def spread(place, sums, own, other, ham, *outs):
     side, size = place[0], SLOTS * BW
     pieces, sums_out = outs[:4], outs[4]
-    sums_out[...] = sums[...]
+    sums_out[...] = sums[...] + brought(other)
     ham[pl.ds(pl.multiple_of(side * size, size), size), :] = own[:size, :]
     ham[pl.ds(pl.multiple_of((1 - side) * size, size), size), :] = other[:size, :]
     mine, others = own[size:, :].astype(F32), other[size : size + META, :].astype(F32)
@@ -290,8 +296,8 @@
 
 
 ROUNDS = (
-    (("layer", 1), ("layer", 2), ("layer", 4), ("ring", 4), ("row", 1), ("row", 2), ("row", 4)),
-    (("side", 1),),
+    (("layer", 1), ("layer", 2), ("layer", 4), ("ring", 4)),
+    (("row", 1), ("row", 2), ("row", 4)),
 )
 
 
@@ -347,8 +353,12 @@
         (VMEM, VMEM),
         moved=2 << 20,
     )(place, ham_pattern, dens_pattern, part, from_other)
-    ham_other = lax.ppermute(ham_own, "side", swap)
     sums = added_over(sums, *ROUNDS[0])
+    held = call(hold, shape(SLOTS * BW + META + CARRIED, BW), [VMEM, VMEM], VMEM, moved=1 << 19)(
+        sums, ham_own
+    )
+    ham_other = lax.ppermute(held, "side", swap)
+
     sizes = [len(REACH[t]) * BW for t in (-1, -1, -2, -2)]
     ham, *pieces, sums = call(
         spread,

time: 252 us -> 250 us (level)
  waiting for transfers between devices: 76 us -> 96.3 us
  starting transfers between devices: 100 us -> 84.7 us
  blocking collectives: 55.4 us -> 49.2 us
    ppermute x1, waiting for transfers between devices: 0.01 us -> 21.1 us  [shards(): ham_other = lax.ppermute(held, 'side', swap)]
    ppermute x8, starting transfers between devices: 33.3 us -> 22.8 us  [exchanged(): got.append(lax.ppermute(piece, LINE, hops + [(b, a) for a, b in hops]))]
    all_to_all x1, blocking collectives: 30.3 us -> 24.1 us  [shards(): lax.all_to_all(answers, 'ring', split_axis=0, concat_axis=0, tiled=True)]
    ppermute x8 -> x7, starting transfers between devices: 30.9 us -> 25.9 us  [added_over(): sums = sums + lax.ppermute(sums, axis, [(i, i ^ step) for i in range(size)])]
    ppermute x8, waiting for transfers between devices: 26 us -> 22.9 us  [exchanged(): got.append(lax.ppermute(piece, LINE, hops + [(b, a) for a, b in hops]))]
    ppermute x8 -> x7, waiting for transfers between devices: 31.8 us -> 34.1 us  [added_over(): sums = sums + lax.ppermute(sums, axis, [(i, i ^ step) for i in range(size)])]
  transfers between devices with their start and end apart: 19 -> 18, of which waited for: 12 -> 11; matrix products, arithmetic and copies ran while one was open for 0% -> 0% of each run, Pallas kernels for 1% -> 1%
where the time goes in v3:
time: 250 us; the launch traced here: 249 us
  waiting for transfers between devices  96.3 us (39%)
  starting transfers between devices  84.7 us (34%)
  blocking collectives  49.2 us (20%)
  Pallas kernels  13.8 us (6%)
  local copies, waits for them, and re-layouts  3.67 us (1%)
    ppermute x7, waiting for transfers between devices, added_over(): sums = sums + lax.ppermute(sums, axis, [(i, i ^ step) for i in range(size)])  34.1 us
    ppermute x7, starting transfers between devices, added_over(): sums = sums + lax.ppermute(sums, axis, [(i, i ^ step) for i in range(size)])  25.9 us
    all_to_all x1, blocking collectives, received(): lax.all_to_all(outgoing, 'ring', split_axis=0, concat_axis=0, tiled=True)  25.1 us
    all_to_all x1, blocking collectives, shards(): lax.all_to_all(answers, 'ring', split_axis=0, concat_axis=0, tiled=True)  24.1 us
    ppermute x8, waiting for transfers between devices, exchanged(): got.append(lax.ppermute(piece, LINE, hops + [(b, a) for a, b in hops]))  22.9 us
    ppermute x8, starting transfers between devices, exchanged(): got.append(lax.ppermute(piece, LINE, hops + [(b, a) for a, b in hops]))  22.8 us
    ppermute x1, waiting for transfers between devices, shards(): ham_other = lax.ppermute(held, 'side', swap)  21.1 us
    ppermute x1, starting transfers between devices, shards(): from_other = lax.ppermute(for_other, 'side', swap)  19.4 us
  transfers between devices with their start and end apart: 18, of which 11 were waited for; matrix products, arithmetic and copies ran while one was open for 0% of the time, Pallas kernels for 1%

profile of v3, /device:TPU:6, one launch (start us, length us, event | category | flops | bytes accessed | tf_op | source)
XLA Modules:
  0.0 248.8 jit_solution(15815270763169130249)
XLA Ops:
  0.7 0.6 copy-done.4
  1.4 1.2 copy-done
  2.6 1.2 copy-done.2
  3.8 2.9 %shard_map.86 = (bf16[8,272,128]{2,1,0:T(8,128)(2,1)S(1)}, bf16[8,272,128]{2,1,0:T(8,128)(2,1)}, s32[16]{0:T(128)S(1)}) custom-call(s32[2]{0:T(128)S(1)} %pad_add_fusion.place, s32[16]{0:T(128)S(1)} %bitcast.5, s32[16]{0:T(128)S(1)} %copy-done.6, f32[16,256]{1,0:T(8,128)S(1)} %copy-done.4, bf16[16,256,128]{2,1,0:T(8,128)(2,1)S(1)} %copy-done, ...), custom_call_target="tpu_custom_call" | custom-call | flops 134217728 | bytes 6291456 | tf_op jit(solution)/shard_map/pallas_call | solution.py:315
  6.8 25.1 %all_to_all.15.arrived = bf16[8,272,128]{2,1,0:T(8,128)(2,1)S(1)} all-to-all(bf16[8,272,128]{2,1,0:T(8,128)(2,1)S(1)} %get-tuple-element.21), channel_id=1, replica_groups=mesh['layer'=8,'row'=8,'ring'=8,'side'=2] {'ring'}, dimensions={0} | all-to-all | bytes 1114112 | tf_op jit(solution)/shard_map/all_to_all | solution.py:329
  31.9 3.5 %all-to-all-start = ((bf16[8,272,128]{2,1,0:T(8,128)(2,1)}), bf16[8,272,128]{2,1,0:T(8,128)(2,1)S(1)}, u32[]{:S(2)}, u32[]{:S(2)}) async-start(bf16[8,272,128]{2,1,0:T(8,128)(2,1)} %get-tuple-element.20), calls=%async_computation | async-start | bytes 1114112 | tf_op jit(solution)/shard_map/all_to_all | solution.py:329
  35.5 0.1 copy.19
  35.6 0.1 copy.20
  35.7 0.1 reshape.19.labels.labels_other
  35.7 0.8 shard_map.88
  36.5 19.4 %collective-permute-start = (bf16[1024,128]{1,0:T(8,128)(2,1)S(1)}, bf16[1024,128]{1,0:T(8,128)(2,1)S(1)}, u32[]{:S(2)}, u32[]{:S(2)}) collective-permute-start(bf16[1024,128]{1,0:T(8,128)(2,1)S(1)} %shard_map.88), channel_id=1, source_target_pairs={{0,1},{1,0},{2,3},{3,2},{4,5},{5,4},{6,7},{7,6},{8,9},{9,8},{10,11... | collective-permute-start | bytes 786440 | tf_op jit(solution)/shard_map/ppermute | solution.py:344
  55.9 0.1 copy.17
  56.0 0.1 copy.18
  56.1 0.1 reshape.18.labels.labels_own
  56.2 0.8 shard_map.87.own
  57.0 18.2 %collective-permute-done.other = bf16[1024,128]{1,0:T(8,128)(2,1)S(1)} collective-permute-done((bf16[1024,128]{1,0:T(8,128)(2,1)S(1)}, bf16[1024,128]{1,0:T(8,128)(2,1)S(1)}, u32[]{:S(2)}, u32[]{:S(2)}) %collective-permute-start) | collective-permute-done | bytes 262176 | tf_op jit(solution)/shard_map/ppermute | solution.py:344
  75.2 0.8 shard_map.89
  76.0 1.9 collective-permute-start.1
  77.9 1.1 collective-permute-done.1
  79.1 2.7 %collective-permute-start.2 = (f32[8,128]{1,0:T(8,128)S(1)}, f32[8,128]{1,0:T(8,128)S(1)}, u32[]{:S(2)}, u32[]{:S(2)}) collective-permute-start(f32[8,128]{1,0:T(8,128)S(1)} %add.29), channel_id=1, source_target_pairs={{0,256},{128,384},{256,0},{384,128},{512,768},{640,896},{768,512},... | collective-permute-start | bytes 12296 | tf_op jit(solution)/shard_map/ppermute | solution.py:294
  81.8 2.8 %collective-permute-done.2 = f32[8,128]{1,0:T(8,128)S(1)} collective-permute-done((f32[8,128]{1,0:T(8,128)S(1)}, f32[8,128]{1,0:T(8,128)S(1)}, u32[]{:S(2)}, u32[]{:S(2)}) %collective-permute-start.2) | collective-permute-done | bytes 4128 | tf_op jit(solution)/shard_map/ppermute | solution.py:294
  84.6 3.3 %collective-permute-start.3 = (f32[8,128]{1,0:T(8,128)S(1)}, f32[8,128]{1,0:T(8,128)S(1)}, u32[]{:S(2)}, u32[]{:S(2)}) collective-permute-start(f32[8,128]{1,0:T(8,128)S(1)} %add.30), channel_id=1, source_target_pairs={{0,512},{128,640},{256,768},{384,896},{512,0},{640,128},{768,256},... | collective-permute-start | bytes 12296 | tf_op jit(solution)/shard_map/ppermute | solution.py:294
  87.9 3.7 %collective-permute-done.3 = f32[8,128]{1,0:T(8,128)S(1)} collective-permute-done((f32[8,128]{1,0:T(8,128)S(1)}, f32[8,128]{1,0:T(8,128)S(1)}, u32[]{:S(2)}, u32[]{:S(2)}) %collective-permute-start.3) | collective-permute-done | bytes 4128 | tf_op jit(solution)/shard_map/ppermute | solution.py:294
  91.6 7.5 %collective-permute-start.4 = (f32[8,128]{1,0:T(8,128)S(1)}, f32[8,128]{1,0:T(8,128)S(1)}, u32[]{:S(2)}, u32[]{:S(2)}) collective-permute-start(f32[8,128]{1,0:T(8,128)S(1)} %add.31), channel_id=1, source_target_pairs={{0,8},{2,10},{4,12},{6,14},{8,0},{10,2},{12,4},{14,6},{1,9},{3,11}... | collective-permute-start | bytes 12296 | tf_op jit(solution)/shard_map/ppermute | solution.py:294
  99.1 1.9 collective-permute-done.4
  101.0 13.1 %collective-permute-start.5 = (bf16[1072,128]{1,0:T(8,128)(2,1)S(1)}, bf16[1072,128]{1,0:T(8,128)(2,1)S(1)}, u32[]{:S(2)}, u32[]{:S(2)}) collective-permute-start(bf16[1072,128]{1,0:T(8,128)(2,1)S(1)} %shard_map.90), channel_id=1, source_target_pairs={{0,1},{1,0},{2,3},{3,2},{4,5},{5,4},{6,7},{7,6},{8,9},{9,8},{10,11... | collective-permute-start | bytes 823304 | tf_op jit(solution)/shard_map/ppermute | solution.py:360
  114.1 21.1 %collective-permute-done.5.other = bf16[1072,128]{1,0:T(8,128)(2,1)S(1)} collective-permute-done((bf16[1072,128]{1,0:T(8,128)(2,1)S(1)}, bf16[1072,128]{1,0:T(8,128)(2,1)S(1)}, u32[]{:S(2)}, u32[]{:S(2)}) %collective-permute-start.5) | collective-permute-done | bytes 274464 | tf_op jit(solution)/shard_map/ppermute | solution.py:360
  135.2 0.7 shard_map.91
  135.9 3.6 %collective-permute-start.9 = (bf16[1680,128]{1,0:T(8,128)(2,1)S(1)}, bf16[1680,128]{1,0:T(8,128)(2,1)S(1)}, u32[]{:S(2)}, u32[]{:S(2)}) collective-permute-start(bf16[1680,128]{1,0:T(8,128)(2,1)S(1)} %get-tuple-element.26), channel_id=1, source_target_pairs={{0,2},{4,6},{8,10},{12,14},{16,18},{20,22},{24,26},{28,30},{32,34}... | collective-permute-start | bytes 1290248 | tf_op jit(solution)/shard_map/ppermute | solution.py:286
  139.5 1.9 collective-permute-start.10
  141.5 4.3 %collective-permute-start.11 = (bf16[1168,128]{1,0:T(8,128)(2,1)S(1)}, bf16[1168,128]{1,0:T(8,128)(2,1)S(1)}, u32[]{:S(2)}, u32[]{:S(2)}) collective-permute-start(bf16[1168,128]{1,0:T(8,128)(2,1)S(1)} %get-tuple-element.28), channel_id=1, source_target_pairs={{0,4},{2,6},{8,12},{10,14},{16,20},{18,22},{24,28},{26,30},{32,36}... | collective-permute-start | bytes 897032 | tf_op jit(solution)/shard_map/ppermute | solution.py:286
  145.7 1.9 collective-permute-start.12
  147.7 6.6 %collective-permute-start.6 = (f32[8,128]{1,0:T(8,128)S(1)}, f32[8,128]{1,0:T(8,128)S(1)}, u32[]{:S(2)}, u32[]{:S(2)}) collective-permute-start(f32[8,128]{1,0:T(8,128)S(1)} %get-tuple-element.24), channel_id=1, source_target_pairs={{0,16},{16,0},{32,48},{48,32},{64,80},{80,64},{96,112},{112,96},{1... | collective-permute-start | bytes 12296 | tf_op jit(solution)/shard_map/ppermute | solution.py:294
  154.3 12.6 %collective-permute-done.6 = f32[8,128]{1,0:T(8,128)S(1)} collective-permute-done((f32[8,128]{1,0:T(8,128)S(1)}, f32[8,128]{1,0:T(8,128)S(1)}, u32[]{:S(2)}, u32[]{:S(2)}) %collective-permute-start.6) | collective-permute-done | bytes 4128 | tf_op jit(solution)/shard_map/ppermute | solution.py:294
  167.0 1.9 collective-permute-start.7
  168.9 4.5 %collective-permute-done.7 = f32[8,128]{1,0:T(8,128)S(1)} collective-permute-done((f32[8,128]{1,0:T(8,128)S(1)}, f32[8,128]{1,0:T(8,128)S(1)}, u32[]{:S(2)}, u32[]{:S(2)}) %collective-permute-start.7) | collective-permute-done | bytes 4128 | tf_op jit(solution)/shard_map/ppermute | solution.py:294
  173.4 1.9 collective-permute-start.8
  175.3 7.5 %collective-permute-done.8 = f32[8,128]{1,0:T(8,128)S(1)} collective-permute-done((f32[8,128]{1,0:T(8,128)S(1)}, f32[8,128]{1,0:T(8,128)S(1)}, u32[]{:S(2)}, u32[]{:S(2)}) %collective-permute-start.8) | collective-permute-done | bytes 4128 | tf_op jit(solution)/shard_map/ppermute | solution.py:294
  182.8 2.2 shard_map.92
  185.0 1.9 collective-permute-start.13
  187.0 1.9 collective-permute-start.14
  188.9 5.4 %collective-permute-start.15 = (bf16[1184,128]{1,0:T(8,128)(2,1)S(1)}, bf16[1184,128]{1,0:T(8,128)(2,1)S(1)}, u32[]{:S(2)}, u32[]{:S(2)}) collective-permute-start(bf16[1184,128]{1,0:T(8,128)(2,1)S(1)} %get-tuple-element.33), channel_id=1, source_target_pairs={{0,4},{2,6},{8,12},{10,14},{16,20},{18,22},{24,28},{26,30},{32,36}... | collective-permute-start | bytes 909320 | tf_op jit(solution)/shard_map/ppermute | solution.py:286
  194.3 1.9 collective-permute-start.16
  196.2 14.2 %collective-permute-done.15.refs_7_ = bf16[1184,128]{1,0:T(8,128)(2,1)S(1)} collective-permute-done((bf16[1184,128]{1,0:T(8,128)(2,1)S(1)}, bf16[1184,128]{1,0:T(8,128)(2,1)S(1)}, u32[]{:S(2)}, u32[]{:S(2)}) %collective-permute-start.15) | collective-permute-done | bytes 303136 | tf_op jit(solution)/shard_map/ppermute | solution.py:286
  210.4 8.7 %collective-permute-done.16.refs_8_ = bf16[1184,128]{1,0:T(8,128)(2,1)S(1)} collective-permute-done((bf16[1184,128]{1,0:T(8,128)(2,1)S(1)}, bf16[1184,128]{1,0:T(8,128)(2,1)S(1)}, u32[]{:S(2)}, u32[]{:S(2)}) %collective-permute-start.16) | collective-permute-done | bytes 303136 | tf_op jit(solution)/shard_map/ppermute | solution.py:286
  219.1 3.5 %shard_map.93 = (bf16[128,1024]{1,0:T(8,128)(2,1)}, bf16[8,512,128]{2,1,0:T(8,128)(2,1)S(1)}) custom-call(s32[2]{0:T(128)S(1)} %pad_add_fusion.place, s32[16]{0:T(128)S(1)} %reshape.18.labels.labels_own, s32[16]{0:T(128)S(1)} %reshape.19.labels.labels_other, f32[8,128]{1,0:T(8,128)S(1)} %add.35.sums, bf16[2064,128]{1,0:T(8,128)(2,1)S(1)} %get-tuple-element.25.ham, ...), custom_call_target="tpu_custom_call" | custom-call | flops 679477248 | bytes 6291456 | tf_op jit(solution)/shard_map/pallas_call | solution.py:386
  222.7 24.1 %all_to_all.16.returned = bf16[8,512,128]{2,1,0:T(8,128)(2,1)S(1)} all-to-all(bf16[8,512,128]{2,1,0:T(8,128)(2,1)S(1)} %get-tuple-element.37), channel_id=1, replica_groups=mesh['layer'=8,'row'=8,'ring'=8,'side'=2] {'ring'}, dimensions={0} | all-to-all | bytes 2097152 | tf_op jit(solution)/shard_map/all_to_all | solution.py:395
  246.8 2.0 shard_map.94
  (35 shorter events, 0.2 us)
Async XLA Ops:
  0.6 0.7 copy-start.4
  0.7 0.7 copy-start.5
  0.7 0.7 copy-start.6
  1.4 1.2 copy-start
  2.6 1.2 copy-start.2
  31.9 24.0 %all-to-all-start = ((bf16[8,272,128]{2,1,0:T(8,128)(2,1)}), bf16[8,272,128]{2,1,0:T(8,128)(2,1)S(1)}, u32[]{:S(2)}, u32[]{:S(2)}) async-start(bf16[8,272,128]{2,1,0:T(8,128)(2,1)} %get-tuple-element.20), calls=%async_computation | async-start | bytes 1114112 | tf_op jit(solution)/shard_map/all_to_all | solution.py:329
  36.5 38.7 %collective-permute-start = (bf16[1024,128]{1,0:T(8,128)(2,1)S(1)}, bf16[1024,128]{1,0:T(8,128)(2,1)S(1)}, u32[]{:S(2)}, u32[]{:S(2)}) collective-permute-start(bf16[1024,128]{1,0:T(8,128)(2,1)S(1)} %shard_map.88), channel_id=1, source_target_pairs={{0,1},{1,0},{2,3},{3,2},{4,5},{5,4},{6,7},{7,6},{8,9},{9,8},{10,11... | collective-permute-start | bytes 786440 | tf_op jit(solution)/shard_map/ppermute | solution.py:344
  56.2 19.0 %copy-start.7 = (s32[1,8]{1,0:T(1,128)S(1)}, s32[1,8]{1,0:T(1,128)}, u32[]{:S(2)}) copy-start(s32[1,8]{1,0:T(1,128)} %ham_pattern.1) | copy-start | bytes 100
  56.2 19.0 %copy-start.8 = (s32[1,8]{1,0:T(1,128)S(1)}, s32[1,8]{1,0:T(1,128)}, u32[]{:S(2)}) copy-start(s32[1,8]{1,0:T(1,128)} %dens_pattern.1) | copy-start | bytes 100
  76.0 3.1 %collective-permute-start.1 = (f32[8,128]{1,0:T(8,128)S(1)}, f32[8,128]{1,0:T(8,128)S(1)}, u32[]{:S(2)}, u32[]{:S(2)}) collective-permute-start(f32[8,128]{1,0:T(8,128)S(1)} %get-tuple-element.22), channel_id=1, source_target_pairs={{0,128},{128,0},{256,384},{384,256},{512,640},{640,512},{768,896},... | collective-permute-start | bytes 12296 | tf_op jit(solution)/shard_map/ppermute | solution.py:294
  79.1 5.5 %collective-permute-start.2 = (f32[8,128]{1,0:T(8,128)S(1)}, f32[8,128]{1,0:T(8,128)S(1)}, u32[]{:S(2)}, u32[]{:S(2)}) collective-permute-start(f32[8,128]{1,0:T(8,128)S(1)} %add.29), channel_id=1, source_target_pairs={{0,256},{128,384},{256,0},{384,128},{512,768},{640,896},{768,512},... | collective-permute-start | bytes 12296 | tf_op jit(solution)/shard_map/ppermute | solution.py:294
  84.6 7.0 %collective-permute-start.3 = (f32[8,128]{1,0:T(8,128)S(1)}, f32[8,128]{1,0:T(8,128)S(1)}, u32[]{:S(2)}, u32[]{:S(2)}) collective-permute-start(f32[8,128]{1,0:T(8,128)S(1)} %add.30), channel_id=1, source_target_pairs={{0,512},{128,640},{256,768},{384,896},{512,0},{640,128},{768,256},... | collective-permute-start | bytes 12296 | tf_op jit(solution)/shard_map/ppermute | solution.py:294
  91.6 9.4 %collective-permute-start.4 = (f32[8,128]{1,0:T(8,128)S(1)}, f32[8,128]{1,0:T(8,128)S(1)}, u32[]{:S(2)}, u32[]{:S(2)}) collective-permute-start(f32[8,128]{1,0:T(8,128)S(1)} %add.31), channel_id=1, source_target_pairs={{0,8},{2,10},{4,12},{6,14},{8,0},{10,2},{12,4},{14,6},{1,9},{3,11}... | collective-permute-start | bytes 12296 | tf_op jit(solution)/shard_map/ppermute | solution.py:294
  101.0 34.2 %collective-permute-start.5 = (bf16[1072,128]{1,0:T(8,128)(2,1)S(1)}, bf16[1072,128]{1,0:T(8,128)(2,1)S(1)}, u32[]{:S(2)}, u32[]{:S(2)}) collective-permute-start(bf16[1072,128]{1,0:T(8,128)(2,1)S(1)} %shard_map.90), channel_id=1, source_target_pairs={{0,1},{1,0},{2,3},{3,2},{4,5},{5,4},{6,7},{7,6},{8,9},{9,8},{10,11... | collective-permute-start | bytes 823304 | tf_op jit(solution)/shard_map/ppermute | solution.py:360
  135.9 46.8 %collective-permute-start.9 = (bf16[1680,128]{1,0:T(8,128)(2,1)S(1)}, bf16[1680,128]{1,0:T(8,128)(2,1)S(1)}, u32[]{:S(2)}, u32[]{:S(2)}) collective-permute-start(bf16[1680,128]{1,0:T(8,128)(2,1)S(1)} %get-tuple-element.26), channel_id=1, source_target_pairs={{0,2},{4,6},{8,10},{12,14},{16,18},{20,22},{24,26},{28,30},{32,34}... | collective-permute-start | bytes 1290248 | tf_op jit(solution)/shard_map/ppermute | solution.py:286
  139.5 43.3 %collective-permute-start.10 = (bf16[1680,128]{1,0:T(8,128)(2,1)S(1)}, bf16[1680,128]{1,0:T(8,128)(2,1)S(1)}, u32[]{:S(2)}, u32[]{:S(2)}) collective-permute-start(bf16[1680,128]{1,0:T(8,128)(2,1)S(1)} %get-tuple-element.27), channel_id=1, source_target_pairs={{2,4},{6,8},{10,12},{14,16},{18,20},{22,24},{26,28},{30,32},{34,36... | collective-permute-start | bytes 1290248 | tf_op jit(solution)/shard_map/ppermute | solution.py:286
  141.5 41.3 %collective-permute-start.11 = (bf16[1168,128]{1,0:T(8,128)(2,1)S(1)}, bf16[1168,128]{1,0:T(8,128)(2,1)S(1)}, u32[]{:S(2)}, u32[]{:S(2)}) collective-permute-start(bf16[1168,128]{1,0:T(8,128)(2,1)S(1)} %get-tuple-element.28), channel_id=1, source_target_pairs={{0,4},{2,6},{8,12},{10,14},{16,20},{18,22},{24,28},{26,30},{32,36}... | collective-permute-start | bytes 897032 | tf_op jit(solution)/shard_map/ppermute | solution.py:286
  145.7 37.0 %collective-permute-start.12 = (bf16[1168,128]{1,0:T(8,128)(2,1)S(1)}, bf16[1168,128]{1,0:T(8,128)(2,1)S(1)}, u32[]{:S(2)}, u32[]{:S(2)}) collective-permute-start(bf16[1168,128]{1,0:T(8,128)(2,1)S(1)} %get-tuple-element.29), channel_id=1, source_target_pairs={{4,8},{6,10},{12,16},{14,18},{20,24},{22,26},{28,32},{30,34},{36,4... | collective-permute-start | bytes 897032 | tf_op jit(solution)/shard_map/ppermute | solution.py:286
  147.7 19.3 %collective-permute-start.6 = (f32[8,128]{1,0:T(8,128)S(1)}, f32[8,128]{1,0:T(8,128)S(1)}, u32[]{:S(2)}, u32[]{:S(2)}) collective-permute-start(f32[8,128]{1,0:T(8,128)S(1)} %get-tuple-element.24), channel_id=1, source_target_pairs={{0,16},{16,0},{32,48},{48,32},{64,80},{80,64},{96,112},{112,96},{1... | collective-permute-start | bytes 12296 | tf_op jit(solution)/shard_map/ppermute | solution.py:294
  167.0 6.4 %collective-permute-start.7 = (f32[8,128]{1,0:T(8,128)S(1)}, f32[8,128]{1,0:T(8,128)S(1)}, u32[]{:S(2)}, u32[]{:S(2)}) collective-permute-start(f32[8,128]{1,0:T(8,128)S(1)} %add.33), channel_id=1, source_target_pairs={{0,32},{16,48},{32,0},{48,16},{64,96},{80,112},{96,64},{112,80},{1... | collective-permute-start | bytes 12296 | tf_op jit(solution)/shard_map/ppermute | solution.py:294
  173.4 9.4 %collective-permute-start.8 = (f32[8,128]{1,0:T(8,128)S(1)}, f32[8,128]{1,0:T(8,128)S(1)}, u32[]{:S(2)}, u32[]{:S(2)}) collective-permute-start(f32[8,128]{1,0:T(8,128)S(1)} %add.34), channel_id=1, source_target_pairs={{0,64},{16,80},{32,96},{48,112},{64,0},{80,16},{96,32},{112,48},{1... | collective-permute-start | bytes 12296 | tf_op jit(solution)/shard_map/ppermute | solution.py:294
  185.0 34.1 %collective-permute-start.13 = (bf16[1696,128]{1,0:T(8,128)(2,1)S(1)}, bf16[1696,128]{1,0:T(8,128)(2,1)S(1)}, u32[]{:S(2)}, u32[]{:S(2)}) collective-permute-start(bf16[1696,128]{1,0:T(8,128)(2,1)S(1)} %get-tuple-element.31), channel_id=1, source_target_pairs={{0,2},{4,6},{8,10},{12,14},{16,18},{20,22},{24,26},{28,30},{32,34}... | collective-permute-start | bytes 1302536 | tf_op jit(solution)/shard_map/ppermute | solution.py:286
  187.0 32.1 %collective-permute-start.14 = (bf16[1696,128]{1,0:T(8,128)(2,1)S(1)}, bf16[1696,128]{1,0:T(8,128)(2,1)S(1)}, u32[]{:S(2)}, u32[]{:S(2)}) collective-permute-start(bf16[1696,128]{1,0:T(8,128)(2,1)S(1)} %get-tuple-element.32), channel_id=1, source_target_pairs={{2,4},{6,8},{10,12},{14,16},{18,20},{22,24},{26,28},{30,32},{34,36... | collective-permute-start | bytes 1302536 | tf_op jit(solution)/shard_map/ppermute | solution.py:286
  188.9 21.5 %collective-permute-start.15 = (bf16[1184,128]{1,0:T(8,128)(2,1)S(1)}, bf16[1184,128]{1,0:T(8,128)(2,1)S(1)}, u32[]{:S(2)}, u32[]{:S(2)}) collective-permute-start(bf16[1184,128]{1,0:T(8,128)(2,1)S(1)} %get-tuple-element.33), channel_id=1, source_target_pairs={{0,4},{2,6},{8,12},{10,14},{16,20},{18,22},{24,28},{26,30},{32,36}... | collective-permute-start | bytes 909320 | tf_op jit(solution)/shard_map/ppermute | solution.py:286
  194.3 24.8 %collective-permute-start.16 = (bf16[1184,128]{1,0:T(8,128)(2,1)S(1)}, bf16[1184,128]{1,0:T(8,128)(2,1)S(1)}, u32[]{:S(2)}, u32[]{:S(2)}) collective-permute-start(bf16[1184,128]{1,0:T(8,128)(2,1)S(1)} %get-tuple-element.34), channel_id=1, source_target_pairs={{4,8},{6,10},{12,16},{14,18},{20,24},{22,26},{28,32},{30,34},{36,4... | collective-permute-start | bytes 909320 | tf_op jit(solution)/shard_map/ppermute | solution.py:286
  222.7 24.1 %copy-start.1 = (bf16[16,256,128]{2,1,0:T(8,128)(2,1)S(1)}, bf16[16,256,128]{2,1,0:T(8,128)(2,1)}, u32[]{:S(2)}) copy-start(bf16[16,256,128]{2,1,0:T(8,128)(2,1)} %prow.3) | copy-start | bytes 3145732
  222.7 24.1 %copy-start.3 = (bf16[16,256,128]{2,1,0:T(8,128)(2,1)S(1)}, bf16[16,256,128]{2,1,0:T(8,128)(2,1)}, u32[]{:S(2)}) copy-start(bf16[16,256,128]{2,1,0:T(8,128)(2,1)} %pcol.3) | copy-start | bytes 3145732
